TPU v7x, 512 devices: a whole 4x4x16 slice. The times are simulated.
512 devices in a mesh: grp: 16 (over y_hi, x, core), seq: 32 (over z, y_lo).
Axes of the slice: x: 4, y: 4 (y_hi: 2, y_lo: 2; y = y_hi * 2 + y_lo), z: 16, core: 2. Of those that a mesh axis runs over, the one named last changes fastest.
Arguments:
- prompt_states: bfloat16 [3072, 5120], P('seq'), may hold values from -6 to 6
- step_states: bfloat16 [4, 16, 5120], replicated, may hold values from -6 to 6
- norm_gain: float32 [5120], replicated, may hold values from 0.1 to 1.9
- w_query: bfloat16 [5120, 8192], P('seq', 'grp'), may hold values from -0.078125 to 0.078125
- key_weight: bfloat16 [5120, 1024], P('seq'), may hold values from -0.078125 to 0.078125
- value_weight: bfloat16 [5120, 1024], P('seq'), may hold values from -0.078125 to 0.078125
- q_gain: float32 [128], replicated, may hold values from 0.5 to 14, as said below
- k_gain: float32 [128], replicated, may hold values from 0.5 to 14, as said below
Outputs:
- prompt_context: bfloat16 [3072, 8192], P('seq', 'grp')
- step_context: bfloat16 [4, 16, 8192], P(None, 'grp', 'seq')
Inputs may be any that keep to these rules, and one draw needn't show every extreme that they name: `q_gain`: positive gain of each query dimension. `k_gain`: positive gain of each key dimension.
All inputs are finite; a program needn't handle non-finite values.
Results may differ from a plain program's by a relative error of at most 0.013.
The roundings to bfloat16 on the way count: a program that leaves them out, or rounds other values in their place, can miss the bound.
Values may be sent and summed in bfloat16 or wider, within the bound.
No kernel may reach another device: no remote copies, remote signals or barrier semaphores. Data moves between devices by JAX's collectives and lax.ppermute only.
A program may use at most 64 MiB of HBM per device.

v0:
```python
import math

import jax
import jax.numpy as jnp
from jax import lax
from jax.sharding import PartitionSpec as P

QUERY_HEADS = 64
KEY_VALUE_HEADS = 8
HEAD_DIM = 128


EPS = 1e-06
THETA = 1000000.0


def rms_scale(values_in, gain):
    return (
        values_in * lax.rsqrt(jnp.mean(values_in * values_in, axis=-1, keepdims=True) + EPS) * gain
    )


def apply_rotary(values_in, positions):
    half_size = values_in.shape[-1] // 2
    freqs = jnp.power(jnp.float32(THETA), -jnp.arange(half_size, dtype=jnp.float32) / half_size)
    angles = positions.astype(jnp.float32)[:, None] * freqs[None, :]
    cosine = jnp.cos(angles)[:, None, :]
    sine = jnp.sin(angles)[:, None, :]
    first_half = values_in[..., :half_size]
    second_half = values_in[..., half_size:]
    return jnp.concatenate(
        [first_half * cosine - second_half * sine, second_half * cosine + first_half * sine],
        axis=-1,
    )


def choose_heads(gathered, lead_shape, kv_total, head_width):
    entries = gathered.shape[-1] // head_width
    repeats = entries // kv_total
    shaped = gathered.reshape(lead_shape + (kv_total, repeats, head_width))
    return shaped[..., 0, :]


def partial_softmax(query_rows, keys_in, values_in, allowed, scaling):
    scores = (
        jnp.einsum("krd,nkd->krn", query_rows, keys_in, preferred_element_type=jnp.float32)
        * scaling
    )
    if allowed is not None:
        scores = jnp.where(allowed[None], scores, -1e30)
    highest = jnp.max(scores, axis=-1)
    weights = jnp.exp(scores - highest[..., None])
    if allowed is not None:
        weights = jnp.where(allowed[None], weights, 0.0)
    weight_sum = jnp.sum(weights, axis=-1)
    summed = jnp.einsum(
        "krn,nkd->krd", weights.astype(jnp.bfloat16), values_in, preferred_element_type=jnp.float32
    )
    return (highest, weight_sum, summed)


def combine_parts(first_part, second_part):
    joined_max = jnp.maximum(first_part[0], second_part[0])
    first_factor = jnp.exp(first_part[0] - joined_max)
    second_factor = jnp.exp(second_part[0] - joined_max)
    weight_sum = first_part[1] * first_factor + second_part[1] * second_factor
    summed = first_part[2] * first_factor[..., None] + second_part[2] * second_factor[..., None]
    return (joined_max, weight_sum, summed)


def history_mask(row_total, response_group, per_kv, decode_steps):
    row_index = jnp.arange(row_total, dtype=jnp.int32)
    row_step = row_index // (response_group * per_kv)
    row_resp = row_index // per_kv % response_group
    key_index = jnp.arange(decode_steps * response_group, dtype=jnp.int32)
    key_step = key_index // response_group
    key_resp = key_index % response_group
    return (row_resp[:, None] == key_resp[None, :]) & (key_step[None, :] <= row_step[:, None])


def shards(
    prompt_states, step_states, norm_gain, w_query, key_weight, value_weight, q_gain, k_gain
):
    seq_count = lax.axis_size("seq")
    grp_count = lax.axis_size("grp")
    seq_index = lax.axis_index("seq")
    grp_index = lax.axis_index("grp")
    head_width = HEAD_DIM
    query_group_width = QUERY_HEADS // KEY_VALUE_HEADS
    scaling = 1.0 / math.sqrt(head_width)
    token_rows = prompt_states.shape[0]
    model_width = prompt_states.shape[1]
    decode_steps = step_states.shape[0]
    responses = step_states.shape[1]
    response_group = responses // grp_count
    prompt_len = token_rows * seq_count
    heads_grp = QUERY_HEADS // grp_count
    kv_grp = max(1, heads_grp // query_group_width)
    per_kv = heads_grp // kv_grp
    first_kv = grp_index * heads_grp // query_group_width
    key_cols = lax.dynamic_slice_in_dim(key_weight, first_kv * head_width, kv_grp * head_width, 1)
    value_cols = lax.dynamic_slice_in_dim(
        value_weight, first_kv * head_width, kv_grp * head_width, 1
    )
    decode_rows = decode_steps * responses
    all_rows = jnp.concatenate(
        [prompt_states, step_states.reshape(decode_rows, model_width)], axis=0
    )
    overall_rows = all_rows.shape[0]
    normalized_input = rms_scale(all_rows.astype(jnp.float32), norm_gain).astype(jnp.bfloat16)
    pieces = (
        lax.all_gather(w_query, "seq", axis=0, tiled=True),
        lax.all_gather(key_cols, "seq", axis=0, tiled=True),
        lax.all_gather(value_cols, "seq", axis=0, tiled=True),
    )
    raw_query, unrotated_key, projected_value = tuple(
        (
            jnp.dot(normalized_input, weight_piece, preferred_element_type=jnp.float32)
            for weight_piece in pieces
        )
    )
    positions = jnp.concatenate(
        [
            seq_index * token_rows + jnp.arange(token_rows, dtype=jnp.int32),
            prompt_len + jnp.arange(decode_rows, dtype=jnp.int32) // responses,
        ]
    )
    query_matrix = apply_rotary(
        rms_scale(raw_query.reshape(overall_rows, heads_grp, head_width), q_gain), positions
    ).astype(jnp.bfloat16)
    keys = apply_rotary(
        rms_scale(unrotated_key.reshape(overall_rows, kv_grp, head_width), k_gain), positions
    ).astype(jnp.bfloat16)
    value_matrix = projected_value.astype(jnp.bfloat16)
    keys = keys.reshape(overall_rows, kv_grp * head_width)
    prompt_q = (
        query_matrix[:token_rows]
        .reshape(token_rows, kv_grp, per_kv, head_width)
        .transpose(1, 2, 0, 3)
        .reshape(kv_grp, per_kv * token_rows, head_width)
    )
    prompt_k = keys[:token_rows]
    prompt_v = value_matrix[:token_rows]
    query_pos = (
        seq_index * token_rows + jnp.arange(per_kv * token_rows, dtype=jnp.int32) % token_rows
    )
    last_pos = seq_index * token_rows + token_rows - 1
    start_attend = (
        jnp.full((kv_grp, per_kv * token_rows), -1e30, jnp.float32),
        jnp.zeros((kv_grp, per_kv * token_rows), jnp.float32),
        jnp.zeros((kv_grp, per_kv * token_rows, head_width), jnp.float32),
    )
    pieces = (
        lax.all_gather(prompt_k, "seq", axis=0, tiled=True),
        lax.all_gather(prompt_v, "seq", axis=0, tiled=True),
    )
    piece_rows = pieces[0].shape[0]

    def compute(state):
        run_max, run_sum, run_acc = state
        key_block = pieces[0].reshape(piece_rows, kv_grp, head_width)
        value_block = pieces[1].reshape(piece_rows, kv_grp, head_width)
        scores = (
            jnp.einsum("krd,nkd->krn", prompt_q, key_block, preferred_element_type=jnp.float32)
            * scaling
        )
        key_pos = jnp.arange(piece_rows, dtype=jnp.int32)
        allowed = key_pos[None, None, :] <= query_pos[None, :, None]
        scores = jnp.where(allowed, scores, -1e30)
        new_max = jnp.maximum(run_max, jnp.max(scores, axis=-1))
        weights = jnp.where(allowed, jnp.exp(scores - new_max[..., None]), 0.0)
        new_sum = jnp.sum(weights, axis=-1)
        new_acc = jnp.einsum(
            "krn,nkd->krd",
            weights.astype(jnp.bfloat16),
            value_block,
            preferred_element_type=jnp.float32,
        )
        return (new_max, new_sum, new_acc)

    final_max, final_sum, final_acc = lax.cond(
        jnp.int32(0) > last_pos, lambda state: state, compute, start_attend
    )
    prompt_out = (
        (final_acc / final_sum[..., None])
        .reshape(kv_grp, per_kv, token_rows, head_width)
        .transpose(2, 0, 1, 3)
    )
    prompt_context = prompt_out.reshape(token_rows, heads_grp * head_width).astype(jnp.bfloat16)
    decode_query = query_matrix[token_rows:].reshape(
        decode_steps, responses, heads_grp * head_width
    )
    step_k = keys[token_rows:].reshape(decode_steps, responses, kv_grp * head_width)
    step_v = value_matrix[token_rows:].reshape(decode_steps, responses, kv_grp * head_width)
    mine_q, local_keys, local_values = (
        lax.all_to_all(decode_query, "grp", split_axis=1, concat_axis=2, tiled=True),
        lax.all_to_all(step_k, "grp", split_axis=1, concat_axis=2, tiled=True),
        lax.all_to_all(step_v, "grp", split_axis=1, concat_axis=2, tiled=True),
    )
    local_keys = choose_heads(
        local_keys, (decode_steps, response_group), KEY_VALUE_HEADS, head_width
    )
    local_values = choose_heads(
        local_values, (decode_steps, response_group), KEY_VALUE_HEADS, head_width
    )
    cached_keys, cached_values = (
        lax.all_gather(prompt_k, "grp", axis=1, tiled=True),
        lax.all_gather(prompt_v, "grp", axis=1, tiled=True),
    )
    cached_keys = choose_heads(cached_keys, (token_rows,), KEY_VALUE_HEADS, head_width)
    cached_values = choose_heads(cached_values, (token_rows,), KEY_VALUE_HEADS, head_width)
    heads_seq = QUERY_HEADS // seq_count
    kv_seq = max(1, heads_seq // query_group_width)
    per_kv_seq = heads_seq // kv_seq
    send_k = jnp.repeat(cached_keys, query_group_width // heads_seq, axis=1)
    send_v = jnp.repeat(cached_values, query_group_width // heads_seq, axis=1)
    held_k, held_v = (
        lax.all_to_all(send_k, "seq", split_axis=1, concat_axis=0, tiled=True),
        lax.all_to_all(send_v, "seq", split_axis=1, concat_axis=0, tiled=True),
    )
    first_kv_seq = seq_index * heads_seq // query_group_width
    own_q = lax.dynamic_slice_in_dim(
        mine_q, seq_index * heads_seq * head_width, heads_seq * head_width, 2
    )
    own_q = own_q.reshape(decode_steps, response_group, kv_seq, per_kv_seq, head_width).transpose(
        2, 0, 1, 3, 4
    )
    own_q = own_q.reshape(kv_seq, decode_steps * response_group * per_kv_seq, head_width)
    hist_k = lax.dynamic_slice_in_dim(local_keys, first_kv_seq, kv_seq, 2).reshape(
        decode_steps * response_group, kv_seq, head_width
    )
    hist_v = lax.dynamic_slice_in_dim(local_values, first_kv_seq, kv_seq, 2).reshape(
        decode_steps * response_group, kv_seq, head_width
    )
    cache_part = partial_softmax(own_q, held_k, held_v, None, scaling)
    allowed = history_mask(own_q.shape[1], response_group, per_kv_seq, decode_steps)
    hist_part = partial_softmax(own_q, hist_k, hist_v, allowed, scaling)
    joined = combine_parts(cache_part, hist_part)
    result = (joined[2] / joined[1][..., None]).reshape(
        kv_seq, decode_steps, response_group, per_kv_seq, head_width
    )
    step_context = (
        result.transpose(1, 2, 0, 3, 4)
        .reshape(decode_steps, response_group, heads_seq * head_width)
        .astype(jnp.bfloat16)
    )
    return (prompt_context, step_context)


def solution(mesh):
    placed = (P("seq", None), P(), P(), P("seq", "grp"), P("seq", None), P("seq", None), P(), P())
    return jax.shard_map(
        shards,
        mesh=mesh,
        in_specs=placed,
        out_specs=(P("seq", "grp"), P(None, "grp", "seq")),
        check_vma=False,
    )
```

profile of v0, /device:TPU:16, one launch (start us, length us, event | category | flops | bytes accessed | tf_op | source)
XLA Modules:
  0.0 668.6 jit_solution(2318286722643510268)
XLA Ops:
  7.2 0.9 copy-done
  8.8 1.4 constant_dynamic-slice_fusion.3
  11.0 1.8 fusion.9
  13.0 133.9 %all-gather.8.cloned.1.call-done = bf16[5120,128]{1,0:T(8,128)(2,1)} async-done(((bf16[160,128]{1,0:T(8,128)(2,1)}), bf16[5120,128]{1,0:T(8,128)(2,1)}) %all-gather.8.cloned.1.call-update) | async-done | bytes 1310736 | tf_op jit(solution)/shard_map/all_gather | solution.py:113
  146.9 2.6 multiply_reduce_fusion.1
  150.7 7.3 %all-to-all-start.3 = ((bf16[4,16,128]{2,0,1:T(4,128)(2,1)}), bf16[4,16,128]{2,0,1:T(4,128)(2,1)S(1)}, u32[]{:S(2)}, u32[]{:S(2)}) async-start(bf16[4,16,128]{2,0,1:T(4,128)(2,1)} %copy.52), calls=%async_computation.3 | async-start | bytes 32768 | tf_op jit(solution)/shard_map/all_to_all | solution.py:197
  158.0 121.9 %all-gather.10.cloned.1.call-done = bf16[5120,128]{1,0:T(8,128)(2,1)} async-done(((bf16[160,128]{1,0:T(8,128)(2,1)}), bf16[5120,128]{1,0:T(8,128)(2,1)}) %all-gather.10.cloned.1.call-update) | async-done | bytes 1310736 | tf_op jit(solution)/shard_map/all_gather | solution.py:114
  279.9 2.0 convolution_convert_fusion
  282.6 7.3 %all-to-all-start.4 = ((bf16[4,16,128]{2,0,1:T(4,128)(2,1)}), bf16[4,16,128]{2,0,1:T(4,128)(2,1)S(1)}, u32[]{:S(2)}, u32[]{:S(2)}) async-start(bf16[4,16,128]{2,0,1:T(4,128)(2,1)} %copy.53), calls=%async_computation.4 | async-start | bytes 32768 | tf_op jit(solution)/shard_map/all_to_all | solution.py:198
  289.9 22.8 %all-gather.1 = bf16[96,1,2048]{2,0,1:T(8,128)(2,1)S(1)} all-gather(bf16[96,1,128]{2,0,1:T(8,128)(2,1)S(1)} %fusion.31), channel_id=3, replica_groups=mesh['grp'=16,'seq'=32] {'grp'}, dimensions={2}, use_global_device_ids=true | all-gather | bytes 417792 | tf_op jit(solution)/shard_map/all_gather | solution.py:207
  313.0 1.0 broadcast_in_dim.29
  314.1 10.5 %all-to-all-start.1 = ((bf16[96,32,128]{2,0,1:T(8,128)(2,1)}), bf16[96,32,128]{2,0,1:T(8,128)(2,1)S(1)}, u32[]{:S(2)}, u32[]{:S(2)}) async-start(bf16[96,32,128]{2,0,1:T(8,128)(2,1)} %bitcast.11), calls=%async_computation.1 | async-start | bytes 1572864 | tf_op jit(solution)/shard_map/all_to_all | solution.py:218
  325.0 128.0 %all-gather.6.cloned.1.call-done = bf16[5120,512]{1,0:T(8,128)(2,1)} async-done(((bf16[160,512]{1,0:T(8,128)(2,1)}), bf16[5120,512]{1,0:T(8,128)(2,1)}) %all-gather.6.cloned.1.call-update) | async-done | bytes 5242896 | tf_op jit(solution)/shard_map/all_gather | solution.py:112
  453.0 3.5 fusion.49
  458.2 5.3 all-to-all-start
  463.6 22.6 %all_gather.27 = bf16[96,2048]{1,0:T(8,128)(2,1)S(1)} all-gather(bf16[96,128]{1,0:T(8,128)(2,1)S(1)} %slice.69), channel_id=1, replica_groups=mesh['grp'=16,'seq'=32] {'grp'}, dimensions={1}, use_global_device_ids=true | all-gather | bytes 417792 | tf_op jit(solution)/shard_map/all_gather | solution.py:208
  486.6 1.0 broadcast_in_dim.30
  487.6 7.8 %all-to-all-start.2 = ((bf16[96,32,128]{2,0,1:T(8,128)(2,1)}), bf16[96,32,128]{2,0,1:T(8,128)(2,1)S(1)}, u32[]{:S(2)}, u32[]{:S(2)}) async-start(bf16[96,32,128]{2,0,1:T(8,128)(2,1)} %bitcast.16), calls=%async_computation.2 | async-start | bytes 1572864 | tf_op jit(solution)/shard_map/all_to_all | solution.py:219
  495.4 94.6 %all-gather = bf16[3072,1,128]{2,0,1:T(8,128)(2,1)S(1)} all-gather(bf16[96,1,128]{2,0,1:T(8,128)(2,1)S(1)} %fusion.31), channel_id=2, replica_groups=mesh['grp'=16,'seq'=32] {'seq'}, dimensions={0}, use_global_device_ids=true | all-gather | bytes 811008 | tf_op jit(solution)/shard_map/all_gather | solution.py:154
  590.0 65.8 %all_gather.25 = bf16[3072,128]{1,0:T(8,128)(2,1)S(1)} all-gather(bf16[96,128]{1,0:T(8,128)(2,1)S(1)} %slice.69), channel_id=1, replica_groups=mesh['grp'=16,'seq'=32] {'seq'}, dimensions={0}, use_global_device_ids=true | all-gather | bytes 811008 | tf_op jit(solution)/shard_map/all_gather | solution.py:155
  655.9 3.4 conditional.1
  655.9 1.1 fusion.53
  657.0 1.0 fusion.4
  658.1 1.2 fusion.1
  (74 shorter events, 9.1 us)
Async XLA Ops:
  7.2 1.0 copy-start
  7.2 139.7 %all-gather.8.cloned.1.call-start = ((), (), s32[]{:S(2)}) async-start(), calls=%async_computation.6 | async-start | bytes 1351680 | tf_op jit(solution)/shard_map/all_gather | solution.py:113
  8.8 271.1 %all-gather.10.cloned.1.call-start = ((), (), s32[]{:S(2)}) async-start(), calls=%async_computation.7 | async-start | bytes 1351680 | tf_op jit(solution)/shard_map/all_gather | solution.py:114
  10.3 442.7 %all-gather.6.cloned.1.call-start = ((), (), s32[]{:S(2)}) async-start(), calls=%async_computation.5 | async-start | bytes 5406720 | tf_op jit(solution)/shard_map/all_gather | solution.py:112
  11.0 138.5 %copy-start.3 = (f32[128]{0:T(128)S(1)}, f32[128]{0:T(128)}, u32[]{:S(2)}) copy-start(f32[128]{0:T(128)} %param.17) | copy-start | bytes 1540
  12.8 267.1 %copy-start.1 = (bf16[96,5120]{1,0:T(8,128)(2,1)S(1)}, bf16[96,5120]{1,0:T(8,128)(2,1)}, u32[]{:S(2)}) copy-start(bf16[96,5120]{1,0:T(8,128)(2,1)} %param.10) | copy-start | bytes 2949124
  12.9 267.1 %copy-start.2 = (bf16[4,16,5120]{2,1,0:T(8,128)(2,1)S(1)}, bf16[4,16,5120]{2,1,0:T(8,128)(2,1)}, u32[]{:S(2)}) copy-start(bf16[4,16,5120]{2,1,0:T(8,128)(2,1)} %param.11) | copy-start | bytes 1966084
  12.9 267.1 %copy-start.5 = (f32[5120]{0:T(1024)S(1)}, f32[5120]{0:T(1024)}, u32[]{:S(2)}) copy-start(f32[5120]{0:T(1024)} %param.12) | copy-start | bytes 61444
  150.7 131.9 %all-to-all-start.3 = ((bf16[4,16,128]{2,0,1:T(4,128)(2,1)}), bf16[4,16,128]{2,0,1:T(4,128)(2,1)S(1)}, u32[]{:S(2)}, u32[]{:S(2)}) async-start(bf16[4,16,128]{2,0,1:T(4,128)(2,1)} %copy.52), calls=%async_computation.3 | async-start | bytes 32768 | tf_op jit(solution)/shard_map/all_to_all | solution.py:197
  282.6 30.4 %all-to-all-start.4 = ((bf16[4,16,128]{2,0,1:T(4,128)(2,1)}), bf16[4,16,128]{2,0,1:T(4,128)(2,1)S(1)}, u32[]{:S(2)}, u32[]{:S(2)}) async-start(bf16[4,16,128]{2,0,1:T(4,128)(2,1)} %copy.53), calls=%async_computation.4 | async-start | bytes 32768 | tf_op jit(solution)/shard_map/all_to_all | solution.py:198
  314.1 144.2 %all-to-all-start.1 = ((bf16[96,32,128]{2,0,1:T(8,128)(2,1)}), bf16[96,32,128]{2,0,1:T(8,128)(2,1)S(1)}, u32[]{:S(2)}, u32[]{:S(2)}) async-start(bf16[96,32,128]{2,0,1:T(8,128)(2,1)} %bitcast.11), calls=%async_computation.1 | async-start | bytes 1572864 | tf_op jit(solution)/shard_map/all_to_all | solution.py:218
  325.0 132.0 %copy-start.4 = (f32[128]{0:T(128)S(1)}, f32[128]{0:T(128)}, u32[]{:S(2)}) copy-start(f32[128]{0:T(128)} %param.16) | copy-start | bytes 1540
  458.2 28.4 %all-to-all-start = ((bf16[4,16,512]{2,0,1:T(4,128)(2,1)}), bf16[4,16,512]{2,0,1:T(4,128)(2,1)S(1)}, u32[]{:S(2)}, u32[]{:S(2)}) async-start(bf16[4,16,512]{2,0,1:T(4,128)(2,1)} %copy.47), calls=%async_computation | async-start | bytes 131072 | tf_op jit(solution)/shard_map/all_to_all | solution.py:196
  487.6 173.4 %all-to-all-start.2 = ((bf16[96,32,128]{2,0,1:T(8,128)(2,1)}), bf16[96,32,128]{2,0,1:T(8,128)(2,1)S(1)}, u32[]{:S(2)}, u32[]{:S(2)}) async-start(bf16[96,32,128]{2,0,1:T(8,128)(2,1)} %bitcast.16), calls=%async_computation.2 | async-start | bytes 1572864 | tf_op jit(solution)/shard_map/all_to_all | solution.py:219
Sparse Core Ops, SparseCore 0:
  10.7 136.2 all-gather.7
  149.0 130.8 all-gather.9
  282.0 170.9 all-gather.5
where the time goes:
time: 669 us
  waiting for transfers between devices  385 us (58%)
  blocking collectives  206 us (31%)
  starting transfers between devices  38.3 us (6%)
  between operations  14.1 us (2%)
  matrix products  11.2 us (2%)
  local copies, waits for them, and re-layouts  9.3 us (1%)
    all_gather x1, waiting for transfers between devices, shards(): lax.all_gather(key_cols, 'seq', axis=0, tiled=True)  134 us
    all_gather x1, waiting for transfers between devices, shards(): lax.all_gather(w_query, 'seq', axis=0, tiled=True)  128 us
    all_gather x1, waiting for transfers between devices, shards(): lax.all_gather(value_cols, 'seq', axis=0, tiled=True)  122 us
    all_gather x1, blocking collectives, shards(): lax.all_gather(prompt_k, 'seq', axis=0, tiled=True)  94.6 us
    all_gather x1, blocking collectives, shards(): lax.all_gather(prompt_v, 'seq', axis=0, tiled=True)  65.8 us
    all_gather x1, blocking collectives, shards(): lax.all_gather(prompt_k, 'grp', axis=1, tiled=True)  22.8 us
    all_gather x1, blocking collectives, shards(): lax.all_gather(prompt_v, 'grp', axis=1, tiled=True)  22.6 us
  transfers between devices with their start and end apart: 8, of which 3 were waited for; matrix products, arithmetic and copies ran while one was open for 3% of the time, Pallas kernels for 0%

commit v1 on v0

v1 whole, which is shorter than its diff:
```python
import math

import jax
import jax.numpy as jnp
from jax import lax
from jax.sharding import PartitionSpec as P

QUERY_HEADS = 64
KEY_VALUE_HEADS = 8
HEAD_DIM = 128
EPS = 1e-06
THETA = 1000000.0
Z = 16
SEQ = 32
GRP = 16

Z_RINGS = [[2 * k + y for k in range(Z)] for y in range(2)]
Y_SWAP = [(i, i ^ 1) for i in range(SEQ)]
CORE_SWAP = [(i, i ^ 1) for i in range(GRP)]
STEP_HOME = [
    (g * SEQ + s, (s // 2) * SEQ + 2 * g + s % 2) for g in range(GRP) for s in range(SEQ)
]


def rms_scale(values_in, gain):
    return (
        values_in * lax.rsqrt(jnp.mean(values_in * values_in, axis=-1, keepdims=True) + EPS) * gain
    )


def rotary_tables(positions):
    half_size = HEAD_DIM // 2
    freqs = jnp.power(jnp.float32(THETA), -jnp.arange(half_size, dtype=jnp.float32) / half_size)
    angles = positions.astype(jnp.float32)[:, None] * freqs[None, :]
    return jnp.cos(angles), jnp.sin(angles)


def rotate(values_in, tables):
    cosine, sine = tables
    half_size = HEAD_DIM // 2
    first_half = values_in[..., :half_size]
    second_half = values_in[..., half_size:]
    return jnp.concatenate(
        [first_half * cosine - second_half * sine, second_half * cosine + first_half * sine],
        axis=-1,
    )


def pick(flag, when_true, when_false):
    return jnp.where(flag, when_true, when_false)


def ordered(flag, first, second, axis):
    return jnp.concatenate([pick(flag, first, second), pick(flag, second, first)], axis=axis)


def gather_z(block):
    return lax.all_gather(block, "seq", axis=0, tiled=True, axis_index_groups=Z_RINGS)


def depth_half(values_in, parity, depth):
    span = 2 * depth
    return jnp.concatenate(
        [
            pick(
                parity == 0,
                values_in[:, span * k : span * k + depth],
                values_in[:, span * k + depth : span * (k + 1)],
            )
            for k in range(Z)
        ],
        axis=1,
    )


def add_halves(partial, rows, steps):
    received = lax.ppermute(partial[: rows + steps], "seq", Y_SWAP)
    return partial[rows:] + jnp.roll(received, steps, axis=0)


def shards(
    prompt_states, step_states, norm_gain, w_query, key_weight, value_weight, q_gain, k_gain
):
    s = lax.axis_index("seq")
    g = lax.axis_index("grp")
    z = s // 2
    y = s % 2
    core = g % 2
    kv_head = g // 2
    rows = prompt_states.shape[0]
    width = prompt_states.shape[1]
    depth = w_query.shape[0]
    steps = step_states.shape[0]
    prompt_len = rows * SEQ
    scaling = 1.0 / math.sqrt(HEAD_DIM)

    q_weight = gather_z(w_query)

    key_cols = lax.dynamic_slice_in_dim(key_weight, kv_head * HEAD_DIM, HEAD_DIM, 1)
    value_cols = lax.dynamic_slice_in_dim(value_weight, kv_head * HEAD_DIM, HEAD_DIM, 1)
    kv_weight = gather_z(pick(core == 0, key_cols, value_cols))

    own_step = lax.dynamic_index_in_dim(step_states, z, 1, keepdims=False)
    x_own = rms_scale(prompt_states.astype(jnp.float32), norm_gain).astype(jnp.bfloat16)
    x_step = rms_scale(own_step.astype(jnp.float32), norm_gain).astype(jnp.bfloat16)
    x_partner = lax.ppermute(depth_half(x_own, 1 - y, depth), "seq", Y_SWAP)
    x_half = jnp.concatenate(
        [x_partner, depth_half(x_step, y, depth), depth_half(x_own, y, depth)], axis=0
    )

    step_pos = prompt_len + jnp.arange(steps, dtype=jnp.int32)
    row_iota = jnp.arange(rows, dtype=jnp.int32)
    own_pos = rows * s + row_iota
    raw_kv = add_halves(
        jnp.dot(x_half, kv_weight, preferred_element_type=jnp.float32), rows, steps
    )
    kv_tables = rotary_tables(jnp.concatenate([step_pos, own_pos]))
    keyed = rotate(rms_scale(raw_kv, k_gain), kv_tables)
    kv_type = pick(core == 0, keyed, raw_kv).astype(jnp.bfloat16)

    own_type = lax.all_to_all(
        jnp.broadcast_to(kv_type[steps:], (Z, rows, HEAD_DIM)),
        "seq",
        split_axis=0,
        concat_axis=0,
        axis_index_groups=Z_RINGS,
        tiled=True,
    ).reshape(Z * rows, HEAD_DIM)
    step_twin = lax.ppermute(kv_type[:steps], "grp", CORE_SWAP)

    own_type, step_twin = lax.optimization_barrier((own_type, step_twin))
    own_twin = lax.ppermute(own_type, "seq", Y_SWAP)
    other_type = lax.ppermute(own_type, "grp", CORE_SWAP)
    x_half, other_type = lax.optimization_barrier((x_half, other_type))
    partial = jnp.dot(x_half, q_weight, preferred_element_type=jnp.float32)
    own_twin, partial = lax.optimization_barrier((own_twin, partial))
    raw_query = add_halves(partial, rows, steps)
    step_heads = lax.dynamic_slice_in_dim(raw_query[:steps], y * 2 * HEAD_DIM, 2 * HEAD_DIM, 1)
    raw_query = jnp.concatenate(
        [
            raw_query[steps:].reshape(rows, 4, HEAD_DIM).transpose(1, 0, 2).reshape(-1, HEAD_DIM),
            step_heads.reshape(steps, 2, HEAD_DIM).transpose(1, 0, 2).reshape(-1, HEAD_DIM),
        ],
        axis=0,
    )
    query_pos = jnp.concatenate([own_pos, own_pos, own_pos, own_pos, step_pos, step_pos])
    query = rotate(rms_scale(raw_query, q_gain), rotary_tables(query_pos)).astype(jnp.bfloat16)

    other_twin = lax.ppermute(own_twin, "grp", CORE_SWAP)
    own_all = jnp.concatenate([own_type, own_twin, kv_type[:steps]], axis=0)
    other_all = jnp.concatenate([other_type, other_twin, step_twin], axis=0)
    cache_keys = pick(core == 0, own_all, other_all)
    cache_values = pick(core == 0, other_all, own_all)
    line = jnp.arange(rows * Z, dtype=jnp.int32)
    line_pos = line + rows * (line // rows)
    key_pos = jnp.concatenate([line_pos + rows * y, line_pos + rows * (1 - y), step_pos])

    scores = (
        jnp.einsum("rd,nd->rn", query, cache_keys, preferred_element_type=jnp.float32)
        * scaling
    )
    allowed = key_pos[None, :] <= query_pos[:, None]
    scores = jnp.where(allowed, scores, -1e30)
    highest = jnp.max(scores, axis=-1, keepdims=True)
    weights = jnp.where(allowed, jnp.exp(scores - highest), 0.0)
    weight_sum = jnp.sum(weights, axis=-1, keepdims=True)
    summed = jnp.dot(
        weights.astype(jnp.bfloat16), cache_values, preferred_element_type=jnp.float32
    )
    context = (summed / weight_sum).astype(jnp.bfloat16)
    prompt_context = context[: 4 * rows].reshape(4, rows, HEAD_DIM).transpose(1, 0, 2)
    step_context = context[4 * rows :].reshape(2, steps, HEAD_DIM).transpose(1, 0, 2)
    half_cols = 2 * HEAD_DIM
    step_out = lax.ppermute(step_context.reshape(steps, half_cols), ("grp", "seq"), STEP_HOME)
    prompt_context = prompt_context.reshape(rows, 4 * HEAD_DIM)
    return (prompt_context, step_out.reshape(steps, 1, half_cols))


def solution(mesh):
    placed = (P("seq", None), P(), P(), P("seq", "grp"), P("seq", None), P("seq", None), P(), P())
    return jax.shard_map(
        shards,
        mesh=mesh,
        in_specs=placed,
        out_specs=(P("seq", "grp"), P(None, "grp", "seq")),
        check_vma=False,
    )
```

time: 669 us -> 152 us (0.23)
  waiting for transfers between devices: 385 us -> 45.8 us
  blocking collectives: 206 us -> 43.6 us
  starting transfers between devices: 38.3 us -> 29.3 us
    all_gather x3 -> x1, waiting for transfers between devices: 384 us -> 0.02 us  [gather_z(): lax.all_gather(block, 'seq', axis=0, tiled=True, axis_index_groups=Z_RINGS)]
    all_gather x4 -> x1, blocking collectives: 206 us -> 43.6 us  [gather_z(): lax.all_gather(block, 'seq', axis=0, tiled=True, axis_index_groups=Z_RINGS)]
    all_to_all x5 -> x1, starting transfers between devices: 38.2 us -> 7.13 us  [shards(): lax.all_to_all(jnp.broadcast_to(kv_type[steps:], (Z, rows, HEAD_DIM)), 's...]
    ppermute x0 -> x8, waiting for transfers between devices: none -> 27.4 us  [the longest x1 9.36 us: shards(): lax.ppermute(step_context.reshape(steps, half_cols), ('grp', 'seq'), STEP...]
    ppermute x0 -> x8, starting transfers between devices: none -> 22.2 us  [the longest x1 6.55 us: shards(): lax.ppermute(step_context.reshape(steps, half_cols), ('grp', 'seq'), STEP...]
    all_to_all x5 -> x1, waiting for transfers between devices: 0.01 us -> 17.7 us  [shards(): lax.all_to_all(jnp.broadcast_to(kv_type[steps:], (Z, rows, HEAD_DIM)), 's...]
  transfers between devices with their start and end apart: 8 -> 10, of which waited for: 3 -> 6; matrix products, arithmetic and copies ran while one was open for 3% -> 9% of each run, Pallas kernels for 0% -> 0%
where the time goes in v1:
time: 152 us
  waiting for transfers between devices  45.8 us (30%)
  blocking collectives  43.6 us (29%)
  starting transfers between devices  29.3 us (19%)
  between operations  14.5 us (10%)
  other arithmetic  9.3 us (6%)
  matrix products  5.47 us (4%)
  local copies, waits for them, and re-layouts  3.42 us (2%)
    all_gather x1, blocking collectives, gather_z(): lax.all_gather(block, 'seq', axis=0, tiled=True, axis_index_groups=Z_RINGS)  43.6 us
    all_to_all x1, waiting for transfers between devices, shards(): lax.all_to_all(jnp.broadcast_to(kv_type[steps:], (Z, rows, HEAD_DIM)), 's...  17.7 us
    ppermute x1, waiting for transfers between devices, shards(): lax.ppermute(step_context.reshape(steps, half_cols), ('grp', 'seq'), STEP...  9.36 us
    ppermute x1, waiting for transfers between devices, shards(): own_twin = lax.ppermute(own_type, 'seq', Y_SWAP)  8.98 us
    ppermute x2, waiting for transfers between devices, add_halves(): received = lax.ppermute(partial[:rows + steps], 'seq', Y_SWAP)  7.98 us
    all_to_all x1, starting transfers between devices, shards(): lax.all_to_all(jnp.broadcast_to(kv_type[steps:], (Z, rows, HEAD_DIM)), 's...  7.13 us
    ppermute x1, starting transfers between devices, shards(): lax.ppermute(step_context.reshape(steps, half_cols), ('grp', 'seq'), STEP...  6.55 us
    ppermute x2, starting transfers between devices, add_halves(): received = lax.ppermute(partial[:rows + steps], 'seq', Y_SWAP)  4.76 us
  transfers between devices with their start and end apart: 10, of which 6 were waited for; matrix products, arithmetic and copies ran while one was open for 9% of the time, Pallas kernels for 0%

profile of v1, /device:TPU:16, one launch (start us, length us, event | category | flops | bytes accessed | tf_op | source)
XLA Modules:
  0.0 151.5 jit_solution(14319662381013786208)
XLA Ops:
  7.9 1.5 fusion.4
  9.4 1.5 %fusion.6 = bf16[96,5120]{1,0:T(8,128)(2,1)S(1)} fusion(bf16[96,5120]{1,0:T(8,128)(2,1)} %param.8, f32[5120]{0:T(1024)} %param.10, f32[96]{0:T(128)S(1)} %add_rsqrt_fusion.3), kind=kLoop, calls=%fused_computation.10 | loop fusion | flops 1966080 | bytes 1986944 | tf_op jit(solution)/shard_map/convert_element_type | solution.py:104
  12.3 3.2 %collective-permute-start = (bf16[96,2560]{1,0:T(8,128)(2,1)S(1)}, bf16[96,2560]{1,0:T(8,128)(2,1)S(1)}, u32[]{:S(2)}, u32[]{:S(2)}) collective-permute-start(bf16[96,2560]{1,0:T(8,128)(2,1)S(1)} %concatenate.55), channel_id=1, source_target_pairs={{0,1},{1,0},{2,3},{3,2},{4,5},{5,4},{6,7},{7,6},{8,9},{9,8},{10,11... | collective-permute-start | bytes 1474568 | tf_op jit(solution)/shard_map/ppermute | solution.py:106
  15.6 1.0 dynamic-slice_convert_fusion
  18.6 43.6 %all_gather.6 = bf16[2560,128]{1,0:T(8,128)(2,1)S(1)} all-gather(bf16[160,128]{1,0:T(8,128)(2,1)S(1)} %dynamic-slice_select_fusion), channel_id=1, replica_groups={{0,2,4,6,8,10,12,14,16,18,20,22,24,26,28,30},{1,3,5,7,9,11,13,15,17,19,..., dimensions={0}, use_global_device_ids=true | all-gather | bytes 696320 | tf_op jit(solution)/shard_map/all_gather | solution.py:58
  62.8 2.6 %collective-permute-start.1 = (f32[100,128]{1,0:T(8,128)S(1)}, f32[100,128]{1,0:T(8,128)S(1)}, u32[]{:S(2)}, u32[]{:S(2)}) collective-permute-start(f32[100,128]{1,0:T(8,128)S(1)} %slice.430), channel_id=1, source_target_pairs={{0,1},{1,0},{2,3},{3,2},{4,5},{5,4},{6,7},{7,6},{8,9},{9,8},{10,11... | collective-permute-start | bytes 153608 | tf_op jit(solution)/shard_map/ppermute | solution.py:77
  65.5 3.4 %collective-permute-done.1 = f32[100,128]{1,0:T(8,128)S(1)} collective-permute-done((f32[100,128]{1,0:T(8,128)S(1)}, f32[100,128]{1,0:T(8,128)S(1)}, u32[]{:S(2)}, u32[]{:S(2)}) %collective-permute-start.1) | collective-permute-done | bytes 51232 | tf_op jit(solution)/shard_map/ppermute | solution.py:77
  70.3 7.1 %all-to-all-start = ((bf16[16,96,128]{2,1,0:T(8,128)(2,1)}), bf16[16,96,128]{2,1,0:T(8,128)(2,1)S(1)}, u32[]{:S(2)}, u32[]{:S(2)}) async-start(bf16[16,96,128]{2,1,0:T(8,128)(2,1)} %broadcast_in_dim.8), calls=%async_computation | async-start | bytes 786432 | tf_op jit(solution)/shard_map/all_to_all | solution.py:121
  77.5 1.9 %collective-permute-start.2 = (bf16[4,128]{1,0:T(4,128)(2,1)S(1)}, bf16[4,128]{1,0:T(4,128)(2,1)S(1)}, u32[]{:S(2)}, u32[]{:S(2)}) collective-permute-start(bf16[4,128]{1,0:T(4,128)(2,1)S(1)} %slice.436), channel_id=1, source_target_pairs={{0,32},{32,0},{64,96},{96,64},{128,160},{160,128},{192,224},{224,1... | collective-permute-start | bytes 3080 | tf_op jit(solution)/shard_map/ppermute | solution.py:129
  79.4 1.1 collective-permute-done.2
  80.5 17.7 %all-to-all-done = bf16[16,96,128]{2,1,0:T(8,128)(2,1)S(1)} async-done(((bf16[16,96,128]{2,1,0:T(8,128)(2,1)}), bf16[16,96,128]{2,1,0:T(8,128)(2,1)S(1)}, u32[]{:S(2)}, u32[]{:S(2)}) %all-to-all-start) | async-done | bytes 393248 | tf_op jit(solution)/shard_map/all_to_all | solution.py:121
  98.2 1.9 %collective-permute-start.4 = (bf16[1536,128]{1,0:T(8,128)(2,1)S(1)}, bf16[1536,128]{1,0:T(8,128)(2,1)S(1)}, u32[]{:S(2)}, u32[]{:S(2)}) collective-permute-start(bf16[1536,128]{1,0:T(8,128)(2,1)S(1)} %bitcast.42), channel_id=1, source_target_pairs={{0,32},{32,0},{64,96},{96,64},{128,160},{160,128},{192,224},{224,1... | collective-permute-start | bytes 1179656 | tf_op jit(solution)/shard_map/ppermute | solution.py:133
  100.2 1.9 %collective-permute-start.3 = (bf16[1536,128]{1,0:T(8,128)(2,1)S(1)}, bf16[1536,128]{1,0:T(8,128)(2,1)S(1)}, u32[]{:S(2)}, u32[]{:S(2)}) collective-permute-start(bf16[1536,128]{1,0:T(8,128)(2,1)S(1)} %bitcast.43), channel_id=1, source_target_pairs={{0,1},{1,0},{2,3},{3,2},{4,5},{5,4},{6,7},{7,6},{8,9},{9,8},{10,11... | collective-permute-start | bytes 1179656 | tf_op jit(solution)/shard_map/ppermute | solution.py:132
  102.2 2.4 %fusion.47 = f32[196,512]{1,0:T(8,128)S(1)} fusion(bf16[196,2560]{1,0:T(8,128)(2,1)S(1)} %pad_maximum_fusion, bf16[2560,512]{1,0:T(8,128)(2,1)} %all-gather.2.cloned.1.call-done), kind=kOutput, calls=%fused_computation.136 | convolution fusion | flops 513802240 | bytes 4026368 | tf_op jit(solution)/shard_map/dot_general | solution.py:135
  104.7 9.0 %collective-permute-done.3 = bf16[1536,128]{1,0:T(8,128)(2,1)S(1)} collective-permute-done((bf16[1536,128]{1,0:T(8,128)(2,1)S(1)}, bf16[1536,128]{1,0:T(8,128)(2,1)S(1)}, u32[]{:S(2)}, u32[]{:S(2)}) %collective-permute-start.3) | collective-permute-done | bytes 393248 | tf_op jit(solution)/shard_map/ppermute | solution.py:132
  113.7 2.2 %collective-permute-start.5 = (f32[100,512]{1,0:T(8,128)S(1)}, f32[100,512]{1,0:T(8,128)S(1)}, u32[]{:S(2)}, u32[]{:S(2)}) collective-permute-start(f32[100,512]{1,0:T(8,128)S(1)} %slice.356), channel_id=1, source_target_pairs={{0,1},{1,0},{2,3},{3,2},{4,5},{5,4},{6,7},{7,6},{8,9},{9,8},{10,11... | collective-permute-start | bytes 614408 | tf_op jit(solution)/shard_map/ppermute | solution.py:77
  115.9 1.9 %collective-permute-start.6 = (bf16[1536,128]{1,0:T(8,128)(2,1)S(1)}, bf16[1536,128]{1,0:T(8,128)(2,1)S(1)}, u32[]{:S(2)}, u32[]{:S(2)}) collective-permute-start(bf16[1536,128]{1,0:T(8,128)(2,1)S(1)} %collective-permute-done.3), channel_id=1, source_target_pairs={{0,32},{32,0},{64,96},{96,64},{128,160},{160,128},{192,224},{224,1... | collective-permute-start | bytes 1179656 | tf_op jit(solution)/shard_map/ppermute | solution.py:149
  117.8 4.6 %collective-permute-done.5 = f32[100,512]{1,0:T(8,128)S(1)} collective-permute-done((f32[100,512]{1,0:T(8,128)S(1)}, f32[100,512]{1,0:T(8,128)S(1)}, u32[]{:S(2)}, u32[]{:S(2)}) %collective-permute-start.5) | collective-permute-done | bytes 204832 | tf_op jit(solution)/shard_map/ppermute | solution.py:77
  122.8 0.8 fusion.22
  123.8 1.4 fusion.45
  125.1 1.1 fusion
  126.3 1.2 fusion.10
  127.5 6.6 %collective-permute-start.7 = (bf16[4,256]{1,0:T(4,128)(2,1)S(1)}, bf16[4,256]{1,0:T(4,128)(2,1)S(1)}, u32[]{:S(2)}, u32[]{:S(2)}) collective-permute-start(bf16[4,256]{1,0:T(4,128)(2,1)S(1)} %bitcast.51), channel_id=1, source_target_pairs={{0,0},{1,1},{2,32},{3,33},{4,64},{5,65},{6,96},{7,97},{8,128},{9,1... | collective-permute-start | bytes 6152 | tf_op jit(solution)/shard_map/ppermute | solution.py:174
  134.8 9.4 %collective-permute-done.7 = bf16[4,256]{1,0:T(4,128)(2,1)S(1)} collective-permute-done((bf16[4,256]{1,0:T(4,128)(2,1)S(1)}, bf16[4,256]{1,0:T(4,128)(2,1)S(1)}, u32[]{:S(2)}, u32[]{:S(2)}) %collective-permute-start.7) | collective-permute-done | bytes 2080 | tf_op jit(solution)/shard_map/ppermute | solution.py:174
  (64 shorter events, 7.9 us)
Async XLA Ops:
  7.2 95.0 %all-gather.2.cloned.1.call-start = ((), (), s32[]{:S(2)}) async-start(), calls=%async_computation.1 | async-start | bytes 2785280 | tf_op jit(solution)/shard_map/all_gather | solution.py:58
  11.2 5.6 %copy-start = (f32[5120]{0:T(1024)S(1)}, f32[5120]{0:T(1024)}, u32[]{:S(2)}) copy-start(f32[5120]{0:T(1024)} %param.10) | copy-start | bytes 61444
  12.3 49.9 %collective-permute-start = (bf16[96,2560]{1,0:T(8,128)(2,1)S(1)}, bf16[96,2560]{1,0:T(8,128)(2,1)S(1)}, u32[]{:S(2)}, u32[]{:S(2)}) collective-permute-start(bf16[96,2560]{1,0:T(8,128)(2,1)S(1)} %concatenate.55), channel_id=1, source_target_pairs={{0,1},{1,0},{2,3},{3,2},{4,5},{5,4},{6,7},{7,6},{8,9},{9,8},{10,11... | collective-permute-start | bytes 1474568 | tf_op jit(solution)/shard_map/ppermute | solution.py:106
  17.7 51.3 %copy-start.1 = (f32[128]{0:T(128)S(1)}, f32[128]{0:T(128)}, u32[]{:S(2)}) copy-start(f32[128]{0:T(128)} %param.15) | copy-start | bytes 1540
  62.8 6.0 %collective-permute-start.1 = (f32[100,128]{1,0:T(8,128)S(1)}, f32[100,128]{1,0:T(8,128)S(1)}, u32[]{:S(2)}, u32[]{:S(2)}) collective-permute-start(f32[100,128]{1,0:T(8,128)S(1)} %slice.430), channel_id=1, source_target_pairs={{0,1},{1,0},{2,3},{3,2},{4,5},{5,4},{6,7},{7,6},{8,9},{9,8},{10,11... | collective-permute-start | bytes 153608 | tf_op jit(solution)/shard_map/ppermute | solution.py:77
  70.3 27.9 %all-to-all-start = ((bf16[16,96,128]{2,1,0:T(8,128)(2,1)}), bf16[16,96,128]{2,1,0:T(8,128)(2,1)S(1)}, u32[]{:S(2)}, u32[]{:S(2)}) async-start(bf16[16,96,128]{2,1,0:T(8,128)(2,1)} %broadcast_in_dim.8), calls=%async_computation | async-start | bytes 786432 | tf_op jit(solution)/shard_map/all_to_all | solution.py:121
  77.5 3.0 %collective-permute-start.2 = (bf16[4,128]{1,0:T(4,128)(2,1)S(1)}, bf16[4,128]{1,0:T(4,128)(2,1)S(1)}, u32[]{:S(2)}, u32[]{:S(2)}) collective-permute-start(bf16[4,128]{1,0:T(4,128)(2,1)S(1)} %slice.436), channel_id=1, source_target_pairs={{0,32},{32,0},{64,96},{96,64},{128,160},{160,128},{192,224},{224,1... | collective-permute-start | bytes 3080 | tf_op jit(solution)/shard_map/ppermute | solution.py:129
  98.2 4.0 %collective-permute-start.4 = (bf16[1536,128]{1,0:T(8,128)(2,1)S(1)}, bf16[1536,128]{1,0:T(8,128)(2,1)S(1)}, u32[]{:S(2)}, u32[]{:S(2)}) collective-permute-start(bf16[1536,128]{1,0:T(8,128)(2,1)S(1)} %bitcast.42), channel_id=1, source_target_pairs={{0,32},{32,0},{64,96},{96,64},{128,160},{160,128},{192,224},{224,1... | collective-permute-start | bytes 1179656 | tf_op jit(solution)/shard_map/ppermute | solution.py:133
  100.2 13.4 %collective-permute-start.3 = (bf16[1536,128]{1,0:T(8,128)(2,1)S(1)}, bf16[1536,128]{1,0:T(8,128)(2,1)S(1)}, u32[]{:S(2)}, u32[]{:S(2)}) collective-permute-start(bf16[1536,128]{1,0:T(8,128)(2,1)S(1)} %bitcast.43), channel_id=1, source_target_pairs={{0,1},{1,0},{2,3},{3,2},{4,5},{5,4},{6,7},{7,6},{8,9},{9,8},{10,11... | collective-permute-start | bytes 1179656 | tf_op jit(solution)/shard_map/ppermute | solution.py:132
  102.2 20.5 %copy-start.2 = (f32[128]{0:T(128)S(1)}, f32[128]{0:T(128)}, u32[]{:S(2)}) copy-start(f32[128]{0:T(128)} %param.14) | copy-start | bytes 1540
  113.7 8.8 %collective-permute-start.5 = (f32[100,512]{1,0:T(8,128)S(1)}, f32[100,512]{1,0:T(8,128)S(1)}, u32[]{:S(2)}, u32[]{:S(2)}) collective-permute-start(f32[100,512]{1,0:T(8,128)S(1)} %slice.356), channel_id=1, source_target_pairs={{0,1},{1,0},{2,3},{3,2},{4,5},{5,4},{6,7},{7,6},{8,9},{9,8},{10,11... | collective-permute-start | bytes 614408 | tf_op jit(solution)/shard_map/ppermute | solution.py:77
  115.9 7.8 %collective-permute-start.6 = (bf16[1536,128]{1,0:T(8,128)(2,1)S(1)}, bf16[1536,128]{1,0:T(8,128)(2,1)S(1)}, u32[]{:S(2)}, u32[]{:S(2)}) collective-permute-start(bf16[1536,128]{1,0:T(8,128)(2,1)S(1)} %collective-permute-done.3), channel_id=1, source_target_pairs={{0,32},{32,0},{64,96},{96,64},{128,160},{160,128},{192,224},{224,1... | collective-permute-start | bytes 1179656 | tf_op jit(solution)/shard_map/ppermute | solution.py:149
  127.5 16.6 %collective-permute-start.7 = (bf16[4,256]{1,0:T(4,128)(2,1)S(1)}, bf16[4,256]{1,0:T(4,128)(2,1)S(1)}, u32[]{:S(2)}, u32[]{:S(2)}) collective-permute-start(bf16[4,256]{1,0:T(4,128)(2,1)S(1)} %bitcast.51), channel_id=1, source_target_pairs={{0,0},{1,1},{2,32},{3,33},{4,64},{5,65},{6,96},{7,97},{8,128},{9,1... | collective-permute-start | bytes 6152 | tf_op jit(solution)/shard_map/ppermute | solution.py:174
Sparse Core Ops, SparseCore 0:
  10.1 89.8 all-gather.1

commit v2 on v1

--- a/solution.py
+++ b/solution.py
@@ -133,7 +133,6 @@
     other_type = lax.ppermute(own_type, "grp", CORE_SWAP)
     x_half, other_type = lax.optimization_barrier((x_half, other_type))
     partial = jnp.dot(x_half, q_weight, preferred_element_type=jnp.float32)
-    own_twin, partial = lax.optimization_barrier((own_twin, partial))
     raw_query = add_halves(partial, rows, steps)
     step_heads = lax.dynamic_slice_in_dim(raw_query[:steps], y * 2 * HEAD_DIM, 2 * HEAD_DIM, 1)
     raw_query = jnp.concatenate(

time: 152 us -> 160 us (1.053)
  waiting for transfers between devices: 45.8 us -> 51.8 us
  matrix products: 5.47 us -> 7.5 us
    ppermute x2, waiting for transfers between devices: 7.98 us -> 10.6 us  [add_halves(): received = lax.ppermute(partial[:rows + steps], 'seq', Y_SWAP)]
    ppermute x1, waiting for transfers between devices: 8.98 us -> 11.5 us  [shards(): own_twin = lax.ppermute(own_type, 'seq', Y_SWAP)]
  transfers between devices with their start and end apart: 10 -> 10, of which waited for: 6 -> 6; matrix products, arithmetic and copies ran while one was open for 9% -> 8% of each run, Pallas kernels for 0% -> 0%
where the time goes in v2:
time: 160 us; the launch traced here: 159 us
  waiting for transfers between devices  51.8 us (32%)
  blocking collectives  43.6 us (27%)
  starting transfers between devices  28.8 us (18%)
  between operations  14.5 us (9%)
  other arithmetic  9.33 us (6%)
  matrix products  7.5 us (5%)
  local copies, waits for them, and re-layouts  3.43 us (2%)
    all_gather x1, blocking collectives, gather_z(): lax.all_gather(block, 'seq', axis=0, tiled=True, axis_index_groups=Z_RINGS)  43.6 us
    all_to_all x1, waiting for transfers between devices, shards(): lax.all_to_all(jnp.broadcast_to(kv_type[steps:], (Z, rows, HEAD_DIM)), 's...  18 us
    ppermute x1, waiting for transfers between devices, shards(): own_twin = lax.ppermute(own_type, 'seq', Y_SWAP)  11.5 us
    ppermute x2, waiting for transfers between devices, add_halves(): received = lax.ppermute(partial[:rows + steps], 'seq', Y_SWAP)  10.6 us
    ppermute x1, waiting for transfers between devices, shards(): lax.ppermute(step_context.reshape(steps, half_cols), ('grp', 'seq'), STEP...  9.85 us
    all_to_all x1, starting transfers between devices, shards(): lax.all_to_all(jnp.broadcast_to(kv_type[steps:], (Z, rows, HEAD_DIM)), 's...  7.14 us
    ppermute x1, starting transfers between devices, shards(): lax.ppermute(step_context.reshape(steps, half_cols), ('grp', 'seq'), STEP...  6.06 us
    ppermute x2, starting transfers between devices, add_halves(): received = lax.ppermute(partial[:rows + steps], 'seq', Y_SWAP)  4.76 us
  transfers between devices with their start and end apart: 10, of which 6 were waited for; matrix products, arithmetic and copies ran while one was open for 8% of the time, Pallas kernels for 0%

profile of v2, /device:TPU:16, one launch (start us, length us, event | category | flops | bytes accessed | tf_op | source)
XLA Modules:
  0.0 159.1 jit_solution(9669885859158361751)
XLA Ops:
  7.9 1.5 fusion.4
  9.4 1.5 fusion.6
  12.3 3.2 %collective-permute-start = (bf16[96,2560]{1,0:T(8,128)(2,1)S(1)}, bf16[96,2560]{1,0:T(8,128)(2,1)S(1)}, u32[]{:S(2)}, u32[]{:S(2)}) collective-permute-start(bf16[96,2560]{1,0:T(8,128)(2,1)S(1)} %concatenate.55), channel_id=1, source_target_pairs={{0,1},{1,0},{2,3},{3,2},{4,5},{5,4},{6,7},{7,6},{8,9},{9,8},{10,11... | collective-permute-start | bytes 1474568 | tf_op jit(solution)/shard_map/ppermute | solution.py:106
  15.6 1.0 dynamic-slice_convert_fusion
  18.6 43.6 %all_gather.6 = bf16[2560,128]{1,0:T(8,128)(2,1)S(1)} all-gather(bf16[160,128]{1,0:T(8,128)(2,1)S(1)} %dynamic-slice_select_fusion), channel_id=1, replica_groups={{0,2,4,6,8,10,12,14,16,18,20,22,24,26,28,30},{1,3,5,7,9,11,13,15,17,19,..., dimensions={0}, use_global_device_ids=true | all-gather | bytes 696320 | tf_op jit(solution)/shard_map/all_gather | solution.py:58
  62.8 2.6 %collective-permute-start.1 = (f32[100,128]{1,0:T(8,128)S(1)}, f32[100,128]{1,0:T(8,128)S(1)}, u32[]{:S(2)}, u32[]{:S(2)}) collective-permute-start(f32[100,128]{1,0:T(8,128)S(1)} %slice.430), channel_id=1, source_target_pairs={{0,1},{1,0},{2,3},{3,2},{4,5},{5,4},{6,7},{7,6},{8,9},{9,8},{10,11... | collective-permute-start | bytes 153608 | tf_op jit(solution)/shard_map/ppermute | solution.py:77
  65.5 3.4 %collective-permute-done.1 = f32[100,128]{1,0:T(8,128)S(1)} collective-permute-done((f32[100,128]{1,0:T(8,128)S(1)}, f32[100,128]{1,0:T(8,128)S(1)}, u32[]{:S(2)}, u32[]{:S(2)}) %collective-permute-start.1) | collective-permute-done | bytes 51232 | tf_op jit(solution)/shard_map/ppermute | solution.py:77
  70.3 7.1 %all-to-all-start = ((bf16[16,96,128]{2,1,0:T(8,128)(2,1)}), bf16[16,96,128]{2,1,0:T(8,128)(2,1)S(1)}, u32[]{:S(2)}, u32[]{:S(2)}) async-start(bf16[16,96,128]{2,1,0:T(8,128)(2,1)} %broadcast_in_dim.8), calls=%async_computation | async-start | bytes 786432 | tf_op jit(solution)/shard_map/all_to_all | solution.py:121
  77.5 1.9 %collective-permute-start.2 = (bf16[4,128]{1,0:T(4,128)(2,1)S(1)}, bf16[4,128]{1,0:T(4,128)(2,1)S(1)}, u32[]{:S(2)}, u32[]{:S(2)}) collective-permute-start(bf16[4,128]{1,0:T(4,128)(2,1)S(1)} %slice.436), channel_id=1, source_target_pairs={{0,32},{32,0},{64,96},{96,64},{128,160},{160,128},{192,224},{224,1... | collective-permute-start | bytes 3080 | tf_op jit(solution)/shard_map/ppermute | solution.py:129
  79.4 1.1 collective-permute-done.2
  80.5 18.0 %all-to-all-done = bf16[16,96,128]{2,1,0:T(8,128)(2,1)S(1)} async-done(((bf16[16,96,128]{2,1,0:T(8,128)(2,1)}), bf16[16,96,128]{2,1,0:T(8,128)(2,1)S(1)}, u32[]{:S(2)}, u32[]{:S(2)}) %all-to-all-start) | async-done | bytes 393248 | tf_op jit(solution)/shard_map/all_to_all | solution.py:121
  98.5 1.9 %collective-permute-start.3 = (bf16[1536,128]{1,0:T(8,128)(2,1)S(1)}, bf16[1536,128]{1,0:T(8,128)(2,1)S(1)}, u32[]{:S(2)}, u32[]{:S(2)}) collective-permute-start(bf16[1536,128]{1,0:T(8,128)(2,1)S(1)} %bitcast.42), channel_id=1, source_target_pairs={{0,32},{32,0},{64,96},{96,64},{128,160},{160,128},{192,224},{224,1... | collective-permute-start | bytes 1179656 | tf_op jit(solution)/shard_map/ppermute | solution.py:133
  100.4 1.9 %collective-permute-start.5 = (bf16[1536,128]{1,0:T(8,128)(2,1)S(1)}, bf16[1536,128]{1,0:T(8,128)(2,1)}, u32[]{:S(2)}, u32[]{:S(2)}) collective-permute-start(bf16[1536,128]{1,0:T(8,128)(2,1)S(1)} %bitcast.43), channel_id=1, source_target_pairs={{0,1},{1,0},{2,3},{3,2},{4,5},{5,4},{6,7},{7,6},{8,9},{9,8},{10,11... | collective-permute-start | bytes 1179656 | tf_op jit(solution)/shard_map/ppermute | solution.py:132
  102.5 11.5 %collective-permute-done.5 = bf16[1536,128]{1,0:T(8,128)(2,1)} collective-permute-done((bf16[1536,128]{1,0:T(8,128)(2,1)S(1)}, bf16[1536,128]{1,0:T(8,128)(2,1)}, u32[]{:S(2)}, u32[]{:S(2)}) %collective-permute-start.5) | collective-permute-done | bytes 393248 | tf_op jit(solution)/shard_map/ppermute | solution.py:132
  114.0 1.9 %collective-permute-start.6 = (bf16[1536,128]{1,0:T(8,128)(2,1)}, bf16[1536,128]{1,0:T(8,128)(2,1)S(1)}, u32[]{:S(2)}, u32[]{:S(2)}) collective-permute-start(bf16[1536,128]{1,0:T(8,128)(2,1)} %collective-permute-done.5), channel_id=1, source_target_pairs={{0,32},{32,0},{64,96},{96,64},{128,160},{160,128},{192,224},{224,1... | collective-permute-start | bytes 1179656 | tf_op jit(solution)/shard_map/ppermute | solution.py:148
  115.9 2.4 %fusion.47 = f32[196,512]{1,0:T(8,128)S(1)} fusion(bf16[196,2560]{1,0:T(8,128)(2,1)S(1)} %pad_maximum_fusion, bf16[2560,512]{1,0:T(8,128)(2,1)} %all-gather.2.cloned.1.call-done), kind=kOutput, calls=%fused_computation.136 | convolution fusion | flops 513802240 | bytes 4026368 | tf_op jit(solution)/shard_map/dot_general | solution.py:135
  118.4 2.2 %collective-permute-start.4 = (f32[100,512]{1,0:T(8,128)S(1)}, f32[100,512]{1,0:T(8,128)S(1)}, u32[]{:S(2)}, u32[]{:S(2)}) collective-permute-start(f32[100,512]{1,0:T(8,128)S(1)} %slice.438), channel_id=1, source_target_pairs={{0,1},{1,0},{2,3},{3,2},{4,5},{5,4},{6,7},{7,6},{8,9},{9,8},{10,11... | collective-permute-start | bytes 614408 | tf_op jit(solution)/shard_map/ppermute | solution.py:77
  120.7 7.3 %collective-permute-done.4 = f32[100,512]{1,0:T(8,128)S(1)} collective-permute-done((f32[100,512]{1,0:T(8,128)S(1)}, f32[100,512]{1,0:T(8,128)S(1)}, u32[]{:S(2)}, u32[]{:S(2)}) %collective-permute-start.4) | collective-permute-done | bytes 204832 | tf_op jit(solution)/shard_map/ppermute | solution.py:77
  128.4 0.8 fusion.22
  129.2 2.4 %fusion.45 = (f32[392]{0:T(512)S(1)}, f32[392,3076]{1,0:T(8,128)S(1)}) fusion(bf16[3076,128]{1,0:T(8,128)(2,1)S(1)} %constant_dynamic-update-slice_fusion, pred[]{:T(512)S(6)} %eq.11, bf16[4,128]{1,0:T(4,128)(2,1)S(1)} %slice.436, bf16[1536,128]{1,0:T(8,128)(2,1)} %collective-permute-done.5, bf16[1536,128]{1,0:T(8,128)(2,1)S(1)} %bitcast.44, ...), kind=kOutput, calls=%fused_computation.134 | convolution fusion | flops 316462336 | bytes 6513873 | tf_op jit(solution)/shard_map/rd,nd->rn/dot_general | solution.py:158
  131.6 1.2 fusion
  132.8 2.3 %fusion.10 = bf16[392,128]{1,0:T(8,128)(2,1)S(1)} fusion(f32[392,3076]{1,0:T(8,128)S(1)} %get-tuple-element.63, f32[392]{0:T(512)S(1)} %get-tuple-element.62, s32[3076]{0:T(1024)S(1)} %pad_add_fusion, s32[392]{0:T(512)S(1)} %concatenate.54, bf16[3076,128]{1,0:T(8,128)(2,1)S(1)} %constant_dynamic-update-slice_fusion, pred[]{:T(512)S(6)} %eq.11, ...), kind=kOutput, calls=%fused_computation.12 | convolution fusion | flops 316362368 | bytes 6515441 | tf_op jit(solution)/shard_map/dot_general | solution.py:166
  135.0 6.1 %collective-permute-start.7 = (bf16[4,256]{1,0:T(4,128)(2,1)S(1)}, bf16[4,256]{1,0:T(4,128)(2,1)S(1)}, u32[]{:S(2)}, u32[]{:S(2)}) collective-permute-start(bf16[4,256]{1,0:T(4,128)(2,1)S(1)} %bitcast.51), channel_id=1, source_target_pairs={{0,0},{1,1},{2,32},{3,33},{4,64},{5,65},{6,96},{7,97},{8,128},{9,1... | collective-permute-start | bytes 6152 | tf_op jit(solution)/shard_map/ppermute | solution.py:173
  141.8 9.8 %collective-permute-done.7 = bf16[4,256]{1,0:T(4,128)(2,1)S(1)} collective-permute-done((bf16[4,256]{1,0:T(4,128)(2,1)S(1)}, bf16[4,256]{1,0:T(4,128)(2,1)S(1)}, u32[]{:S(2)}, u32[]{:S(2)}) %collective-permute-start.7) | collective-permute-done | bytes 2080 | tf_op jit(solution)/shard_map/ppermute | solution.py:173
  (64 shorter events, 7.9 us)
Async XLA Ops:
  7.2 108.8 %all-gather.2.cloned.1.call-start = ((), (), s32[]{:S(2)}) async-start(), calls=%async_computation.1 | async-start | bytes 2785280 | tf_op jit(solution)/shard_map/all_gather | solution.py:58
  11.2 5.6 %copy-start = (f32[5120]{0:T(1024)S(1)}, f32[5120]{0:T(1024)}, u32[]{:S(2)}) copy-start(f32[5120]{0:T(1024)} %param.10) | copy-start | bytes 61444
  12.3 49.9 %collective-permute-start = (bf16[96,2560]{1,0:T(8,128)(2,1)S(1)}, bf16[96,2560]{1,0:T(8,128)(2,1)S(1)}, u32[]{:S(2)}, u32[]{:S(2)}) collective-permute-start(bf16[96,2560]{1,0:T(8,128)(2,1)S(1)} %concatenate.55), channel_id=1, source_target_pairs={{0,1},{1,0},{2,3},{3,2},{4,5},{5,4},{6,7},{7,6},{8,9},{9,8},{10,11... | collective-permute-start | bytes 1474568 | tf_op jit(solution)/shard_map/ppermute | solution.py:106
  17.7 51.3 %copy-start.1 = (f32[128]{0:T(128)S(1)}, f32[128]{0:T(128)}, u32[]{:S(2)}) copy-start(f32[128]{0:T(128)} %param.15) | copy-start | bytes 1540
  62.8 6.0 %collective-permute-start.1 = (f32[100,128]{1,0:T(8,128)S(1)}, f32[100,128]{1,0:T(8,128)S(1)}, u32[]{:S(2)}, u32[]{:S(2)}) collective-permute-start(f32[100,128]{1,0:T(8,128)S(1)} %slice.430), channel_id=1, source_target_pairs={{0,1},{1,0},{2,3},{3,2},{4,5},{5,4},{6,7},{7,6},{8,9},{9,8},{10,11... | collective-permute-start | bytes 153608 | tf_op jit(solution)/shard_map/ppermute | solution.py:77
  70.3 28.2 %all-to-all-start = ((bf16[16,96,128]{2,1,0:T(8,128)(2,1)}), bf16[16,96,128]{2,1,0:T(8,128)(2,1)S(1)}, u32[]{:S(2)}, u32[]{:S(2)}) async-start(bf16[16,96,128]{2,1,0:T(8,128)(2,1)} %broadcast_in_dim.8), calls=%async_computation | async-start | bytes 786432 | tf_op jit(solution)/shard_map/all_to_all | solution.py:121
  77.5 3.0 %collective-permute-start.2 = (bf16[4,128]{1,0:T(4,128)(2,1)S(1)}, bf16[4,128]{1,0:T(4,128)(2,1)S(1)}, u32[]{:S(2)}, u32[]{:S(2)}) collective-permute-start(bf16[4,128]{1,0:T(4,128)(2,1)S(1)} %slice.436), channel_id=1, source_target_pairs={{0,32},{32,0},{64,96},{96,64},{128,160},{160,128},{192,224},{224,1... | collective-permute-start | bytes 3080 | tf_op jit(solution)/shard_map/ppermute | solution.py:129
  98.5 4.0 %collective-permute-start.3 = (bf16[1536,128]{1,0:T(8,128)(2,1)S(1)}, bf16[1536,128]{1,0:T(8,128)(2,1)S(1)}, u32[]{:S(2)}, u32[]{:S(2)}) collective-permute-start(bf16[1536,128]{1,0:T(8,128)(2,1)S(1)} %bitcast.42), channel_id=1, source_target_pairs={{0,32},{32,0},{64,96},{96,64},{128,160},{160,128},{192,224},{224,1... | collective-permute-start | bytes 1179656 | tf_op jit(solution)/shard_map/ppermute | solution.py:133
  100.4 13.5 %collective-permute-start.5 = (bf16[1536,128]{1,0:T(8,128)(2,1)S(1)}, bf16[1536,128]{1,0:T(8,128)(2,1)}, u32[]{:S(2)}, u32[]{:S(2)}) collective-permute-start(bf16[1536,128]{1,0:T(8,128)(2,1)S(1)} %bitcast.43), channel_id=1, source_target_pairs={{0,1},{1,0},{2,3},{3,2},{4,5},{5,4},{6,7},{7,6},{8,9},{9,8},{10,11... | collective-permute-start | bytes 1179656 | tf_op jit(solution)/shard_map/ppermute | solution.py:132
  114.0 6.7 %collective-permute-start.6 = (bf16[1536,128]{1,0:T(8,128)(2,1)}, bf16[1536,128]{1,0:T(8,128)(2,1)S(1)}, u32[]{:S(2)}, u32[]{:S(2)}) collective-permute-start(bf16[1536,128]{1,0:T(8,128)(2,1)} %collective-permute-done.5), channel_id=1, source_target_pairs={{0,32},{32,0},{64,96},{96,64},{128,160},{160,128},{192,224},{224,1... | collective-permute-start | bytes 1179656 | tf_op jit(solution)/shard_map/ppermute | solution.py:148
  118.4 9.9 %copy-start.2 = (f32[128]{0:T(128)S(1)}, f32[128]{0:T(128)}, u32[]{:S(2)}) copy-start(f32[128]{0:T(128)} %param.14) | copy-start | bytes 1540
  118.4 9.5 %collective-permute-start.4 = (f32[100,512]{1,0:T(8,128)S(1)}, f32[100,512]{1,0:T(8,128)S(1)}, u32[]{:S(2)}, u32[]{:S(2)}) collective-permute-start(f32[100,512]{1,0:T(8,128)S(1)} %slice.438), channel_id=1, source_target_pairs={{0,1},{1,0},{2,3},{3,2},{4,5},{5,4},{6,7},{7,6},{8,9},{9,8},{10,11... | collective-permute-start | bytes 614408 | tf_op jit(solution)/shard_map/ppermute | solution.py:77
  135.0 16.6 %collective-permute-start.7 = (bf16[4,256]{1,0:T(4,128)(2,1)S(1)}, bf16[4,256]{1,0:T(4,128)(2,1)S(1)}, u32[]{:S(2)}, u32[]{:S(2)}) collective-permute-start(bf16[4,256]{1,0:T(4,128)(2,1)S(1)} %bitcast.51), channel_id=1, source_target_pairs={{0,0},{1,1},{2,32},{3,33},{4,64},{5,65},{6,96},{7,97},{8,128},{9,1... | collective-permute-start | bytes 6152 | tf_op jit(solution)/shard_map/ppermute | solution.py:173
Sparse Core Ops, SparseCore 0:
  10.1 89.9 all-gather.1

commit v3 on v2

--- a/solution.py
+++ b/solution.py
@@ -133,7 +133,7 @@
     other_type = lax.ppermute(own_type, "grp", CORE_SWAP)
     x_half, other_type = lax.optimization_barrier((x_half, other_type))
     partial = jnp.dot(x_half, q_weight, preferred_element_type=jnp.float32)
-    raw_query = add_halves(partial, rows, steps)
+    own_twin, raw_query = lax.optimization_barrier((own_twin, add_halves(partial, rows, steps)))
     step_heads = lax.dynamic_slice_in_dim(raw_query[:steps], y * 2 * HEAD_DIM, 2 * HEAD_DIM, 1)
     raw_query = jnp.concatenate(
         [

time: 160 us -> 151 us (0.944)
  waiting for transfers between devices: 51.8 us -> 42.5 us
  starting transfers between devices: 28.8 us -> 31.1 us
  matrix products: 7.5 us -> 5.46 us
    ppermute x1, waiting for transfers between devices: 11.5 us -> 0.01 us  [shards(): own_twin = lax.ppermute(own_type, 'seq', Y_SWAP)]
    ppermute x2, waiting for transfers between devices: 10.6 us -> 13 us  [add_halves(): received = lax.ppermute(partial[:rows + steps], 'seq', Y_SWAP)]
    ppermute x2, starting transfers between devices: 4.76 us -> 6.48 us  [add_halves(): received = lax.ppermute(partial[:rows + steps], 'seq', Y_SWAP)]
  transfers between devices with their start and end apart: 10 -> 10, of which waited for: 6 -> 6; matrix products, arithmetic and copies ran while one was open for 8% -> 9% of each run, Pallas kernels for 0% -> 0%
where the time goes in v3:
time: 151 us; the launch traced here: 150 us
  blocking collectives  43.6 us (29%)
  waiting for transfers between devices  42.5 us (28%)
  starting transfers between devices  31.1 us (21%)
  between operations  14.5 us (10%)
  other arithmetic  9.3 us (6%)
  matrix products  5.46 us (4%)
  local copies, waits for them, and re-layouts  3.42 us (2%)
    all_gather x1, blocking collectives, gather_z(): lax.all_gather(block, 'seq', axis=0, tiled=True, axis_index_groups=Z_RINGS)  43.6 us
    all_to_all x1, waiting for transfers between devices, shards(): lax.all_to_all(jnp.broadcast_to(kv_type[steps:], (Z, rows, HEAD_DIM)), 's...  17.7 us
    ppermute x2, waiting for transfers between devices, add_halves(): received = lax.ppermute(partial[:rows + steps], 'seq', Y_SWAP)  13 us
    ppermute x1, waiting for transfers between devices, shards(): lax.ppermute(step_context.reshape(steps, half_cols), ('grp', 'seq'), STEP...  9.34 us
    all_to_all x1, starting transfers between devices, shards(): lax.all_to_all(jnp.broadcast_to(kv_type[steps:], (Z, rows, HEAD_DIM)), 's...  7.13 us
    ppermute x1, starting transfers between devices, shards(): lax.ppermute(step_context.reshape(steps, half_cols), ('grp', 'seq'), STEP...  6.57 us
    ppermute x2, starting transfers between devices, add_halves(): received = lax.ppermute(partial[:rows + steps], 'seq', Y_SWAP)  6.48 us
    ppermute x1, starting transfers between devices, shards(): x_partner = lax.ppermute(depth_half(x_own, 1 - y, depth), 'seq', Y_SWAP)  3.19 us
  transfers between devices with their start and end apart: 10, of which 6 were waited for; matrix products, arithmetic and copies ran while one was open for 9% of the time, Pallas kernels for 0%

profile of v3, /device:TPU:16, one launch (start us, length us, event | category | flops | bytes accessed | tf_op | source)
XLA Modules:
  0.0 150.0 jit_solution(15511758012351612966)
XLA Ops:
  7.9 1.5 fusion.4
  9.4 1.5 %fusion.6 = bf16[96,5120]{1,0:T(8,128)(2,1)S(1)} fusion(bf16[96,5120]{1,0:T(8,128)(2,1)} %param.8, f32[5120]{0:T(1024)} %param.10, f32[96]{0:T(128)S(1)} %add_rsqrt_fusion.3), kind=kLoop, calls=%fused_computation.10 | loop fusion | flops 1966080 | bytes 1986944 | tf_op jit(solution)/shard_map/convert_element_type | solution.py:104
  12.3 3.2 %collective-permute-start = (bf16[96,2560]{1,0:T(8,128)(2,1)S(1)}, bf16[96,2560]{1,0:T(8,128)(2,1)S(1)}, u32[]{:S(2)}, u32[]{:S(2)}) collective-permute-start(bf16[96,2560]{1,0:T(8,128)(2,1)S(1)} %concatenate.55), channel_id=1, source_target_pairs={{0,1},{1,0},{2,3},{3,2},{4,5},{5,4},{6,7},{7,6},{8,9},{9,8},{10,11... | collective-permute-start | bytes 1474568 | tf_op jit(solution)/shard_map/ppermute | solution.py:106
  15.6 1.0 dynamic-slice_convert_fusion
  17.8 0.8 dynamic-slice_select_fusion
  18.6 43.6 %all_gather.6 = bf16[2560,128]{1,0:T(8,128)(2,1)S(1)} all-gather(bf16[160,128]{1,0:T(8,128)(2,1)S(1)} %dynamic-slice_select_fusion), channel_id=1, replica_groups={{0,2,4,6,8,10,12,14,16,18,20,22,24,26,28,30},{1,3,5,7,9,11,13,15,17,19,..., dimensions={0}, use_global_device_ids=true | all-gather | bytes 696320 | tf_op jit(solution)/shard_map/all_gather | solution.py:58
  62.8 2.6 %collective-permute-start.1 = (f32[100,128]{1,0:T(8,128)S(1)}, f32[100,128]{1,0:T(8,128)S(1)}, u32[]{:S(2)}, u32[]{:S(2)}) collective-permute-start(f32[100,128]{1,0:T(8,128)S(1)} %slice.430), channel_id=1, source_target_pairs={{0,1},{1,0},{2,3},{3,2},{4,5},{5,4},{6,7},{7,6},{8,9},{9,8},{10,11... | collective-permute-start | bytes 153608 | tf_op jit(solution)/shard_map/ppermute | solution.py:77
  65.5 3.4 %collective-permute-done.1 = f32[100,128]{1,0:T(8,128)S(1)} collective-permute-done((f32[100,128]{1,0:T(8,128)S(1)}, f32[100,128]{1,0:T(8,128)S(1)}, u32[]{:S(2)}, u32[]{:S(2)}) %collective-permute-start.1) | collective-permute-done | bytes 51232 | tf_op jit(solution)/shard_map/ppermute | solution.py:77
  70.3 7.1 %all-to-all-start = ((bf16[16,96,128]{2,1,0:T(8,128)(2,1)}), bf16[16,96,128]{2,1,0:T(8,128)(2,1)S(1)}, u32[]{:S(2)}, u32[]{:S(2)}) async-start(bf16[16,96,128]{2,1,0:T(8,128)(2,1)} %broadcast_in_dim.8), calls=%async_computation | async-start | bytes 786432 | tf_op jit(solution)/shard_map/all_to_all | solution.py:121
  77.5 1.9 %collective-permute-start.2 = (bf16[4,128]{1,0:T(4,128)(2,1)S(1)}, bf16[4,128]{1,0:T(4,128)(2,1)S(1)}, u32[]{:S(2)}, u32[]{:S(2)}) collective-permute-start(bf16[4,128]{1,0:T(4,128)(2,1)S(1)} %slice.436), channel_id=1, source_target_pairs={{0,32},{32,0},{64,96},{96,64},{128,160},{160,128},{192,224},{224,1... | collective-permute-start | bytes 3080 | tf_op jit(solution)/shard_map/ppermute | solution.py:129
  79.4 1.1 collective-permute-done.2
  80.5 17.7 %all-to-all-done = bf16[16,96,128]{2,1,0:T(8,128)(2,1)S(1)} async-done(((bf16[16,96,128]{2,1,0:T(8,128)(2,1)}), bf16[16,96,128]{2,1,0:T(8,128)(2,1)S(1)}, u32[]{:S(2)}, u32[]{:S(2)}) %all-to-all-start) | async-done | bytes 393248 | tf_op jit(solution)/shard_map/all_to_all | solution.py:121
  98.2 1.9 %collective-permute-start.4 = (bf16[1536,128]{1,0:T(8,128)(2,1)S(1)}, bf16[1536,128]{1,0:T(8,128)(2,1)S(1)}, u32[]{:S(2)}, u32[]{:S(2)}) collective-permute-start(bf16[1536,128]{1,0:T(8,128)(2,1)S(1)} %bitcast.42), channel_id=1, source_target_pairs={{0,32},{32,0},{64,96},{96,64},{128,160},{160,128},{192,224},{224,1... | collective-permute-start | bytes 1179656 | tf_op jit(solution)/shard_map/ppermute | solution.py:133
  100.3 1.9 %collective-permute-start.3 = (bf16[1536,128]{1,0:T(8,128)(2,1)S(1)}, bf16[1536,128]{1,0:T(8,128)(2,1)S(1)}, u32[]{:S(2)}, u32[]{:S(2)}) collective-permute-start(bf16[1536,128]{1,0:T(8,128)(2,1)S(1)} %bitcast.43), channel_id=1, source_target_pairs={{0,1},{1,0},{2,3},{3,2},{4,5},{5,4},{6,7},{7,6},{8,9},{9,8},{10,11... | collective-permute-start | bytes 1179656 | tf_op jit(solution)/shard_map/ppermute | solution.py:132
  102.2 2.4 %fusion.47 = f32[196,512]{1,0:T(8,128)S(1)} fusion(bf16[196,2560]{1,0:T(8,128)(2,1)S(1)} %pad_maximum_fusion, bf16[2560,512]{1,0:T(8,128)(2,1)} %all-gather.2.cloned.1.call-done), kind=kOutput, calls=%fused_computation.136 | convolution fusion | flops 513802240 | bytes 4026368 | tf_op jit(solution)/shard_map/dot_general | solution.py:135
  104.7 3.9 %collective-permute-start.5 = (f32[100,512]{1,0:T(8,128)S(1)}, f32[100,512]{1,0:T(8,128)S(1)}, u32[]{:S(2)}, u32[]{:S(2)}) collective-permute-start(f32[100,512]{1,0:T(8,128)S(1)} %slice.438), channel_id=1, source_target_pairs={{0,1},{1,0},{2,3},{3,2},{4,5},{5,4},{6,7},{7,6},{8,9},{9,8},{10,11... | collective-permute-start | bytes 614408 | tf_op jit(solution)/shard_map/ppermute | solution.py:77
  108.6 9.6 %collective-permute-done.5 = f32[100,512]{1,0:T(8,128)S(1)} collective-permute-done((f32[100,512]{1,0:T(8,128)S(1)}, f32[100,512]{1,0:T(8,128)S(1)}, u32[]{:S(2)}, u32[]{:S(2)}) %collective-permute-start.5) | collective-permute-done | bytes 204832 | tf_op jit(solution)/shard_map/ppermute | solution.py:77
  118.5 1.9 %collective-permute-start.6 = (bf16[1536,128]{1,0:T(8,128)(2,1)S(1)}, bf16[1536,128]{1,0:T(8,128)(2,1)S(1)}, u32[]{:S(2)}, u32[]{:S(2)}) collective-permute-start(bf16[1536,128]{1,0:T(8,128)(2,1)S(1)} %collective-permute-done.3), channel_id=1, source_target_pairs={{0,32},{32,0},{64,96},{96,64},{128,160},{160,128},{192,224},{224,1... | collective-permute-start | bytes 1179656 | tf_op jit(solution)/shard_map/ppermute | solution.py:148
  120.6 0.8 fusion.22
  122.2 1.4 fusion.45
  123.6 1.1 fusion
  124.7 1.2 fusion.10
  125.9 6.6 %collective-permute-start.7 = (bf16[4,256]{1,0:T(4,128)(2,1)S(1)}, bf16[4,256]{1,0:T(4,128)(2,1)S(1)}, u32[]{:S(2)}, u32[]{:S(2)}) collective-permute-start(bf16[4,256]{1,0:T(4,128)(2,1)S(1)} %bitcast.51), channel_id=1, source_target_pairs={{0,0},{1,1},{2,32},{3,33},{4,64},{5,65},{6,96},{7,97},{8,128},{9,1... | collective-permute-start | bytes 6152 | tf_op jit(solution)/shard_map/ppermute | solution.py:173
  133.2 9.3 %collective-permute-done.7 = bf16[4,256]{1,0:T(4,128)(2,1)S(1)} collective-permute-done((bf16[4,256]{1,0:T(4,128)(2,1)S(1)}, bf16[4,256]{1,0:T(4,128)(2,1)S(1)}, u32[]{:S(2)}, u32[]{:S(2)}) %collective-permute-start.7) | collective-permute-done | bytes 2080 | tf_op jit(solution)/shard_map/ppermute | solution.py:173
  (64 shorter events, 7.8 us)
Async XLA Ops:
  7.2 95.0 %all-gather.2.cloned.1.call-start = ((), (), s32[]{:S(2)}) async-start(), calls=%async_computation.1 | async-start | bytes 2785280 | tf_op jit(solution)/shard_map/all_gather | solution.py:58
  11.2 5.6 %copy-start = (f32[5120]{0:T(1024)S(1)}, f32[5120]{0:T(1024)}, u32[]{:S(2)}) copy-start(f32[5120]{0:T(1024)} %param.10) | copy-start | bytes 61444
  12.3 49.9 %collective-permute-start = (bf16[96,2560]{1,0:T(8,128)(2,1)S(1)}, bf16[96,2560]{1,0:T(8,128)(2,1)S(1)}, u32[]{:S(2)}, u32[]{:S(2)}) collective-permute-start(bf16[96,2560]{1,0:T(8,128)(2,1)S(1)} %concatenate.55), channel_id=1, source_target_pairs={{0,1},{1,0},{2,3},{3,2},{4,5},{5,4},{6,7},{7,6},{8,9},{9,8},{10,11... | collective-permute-start | bytes 1474568 | tf_op jit(solution)/shard_map/ppermute | solution.py:106
  17.7 51.3 %copy-start.1 = (f32[128]{0:T(128)S(1)}, f32[128]{0:T(128)}, u32[]{:S(2)}) copy-start(f32[128]{0:T(128)} %param.15) | copy-start | bytes 1540
  62.8 6.0 %collective-permute-start.1 = (f32[100,128]{1,0:T(8,128)S(1)}, f32[100,128]{1,0:T(8,128)S(1)}, u32[]{:S(2)}, u32[]{:S(2)}) collective-permute-start(f32[100,128]{1,0:T(8,128)S(1)} %slice.430), channel_id=1, source_target_pairs={{0,1},{1,0},{2,3},{3,2},{4,5},{5,4},{6,7},{7,6},{8,9},{9,8},{10,11... | collective-permute-start | bytes 153608 | tf_op jit(solution)/shard_map/ppermute | solution.py:77
  70.3 27.9 %all-to-all-start = ((bf16[16,96,128]{2,1,0:T(8,128)(2,1)}), bf16[16,96,128]{2,1,0:T(8,128)(2,1)S(1)}, u32[]{:S(2)}, u32[]{:S(2)}) async-start(bf16[16,96,128]{2,1,0:T(8,128)(2,1)} %broadcast_in_dim.8), calls=%async_computation | async-start | bytes 786432 | tf_op jit(solution)/shard_map/all_to_all | solution.py:121
  77.5 3.0 %collective-permute-start.2 = (bf16[4,128]{1,0:T(4,128)(2,1)S(1)}, bf16[4,128]{1,0:T(4,128)(2,1)S(1)}, u32[]{:S(2)}, u32[]{:S(2)}) collective-permute-start(bf16[4,128]{1,0:T(4,128)(2,1)S(1)} %slice.436), channel_id=1, source_target_pairs={{0,32},{32,0},{64,96},{96,64},{128,160},{160,128},{192,224},{224,1... | collective-permute-start | bytes 3080 | tf_op jit(solution)/shard_map/ppermute | solution.py:129
  98.2 4.0 %collective-permute-start.4 = (bf16[1536,128]{1,0:T(8,128)(2,1)S(1)}, bf16[1536,128]{1,0:T(8,128)(2,1)S(1)}, u32[]{:S(2)}, u32[]{:S(2)}) collective-permute-start(bf16[1536,128]{1,0:T(8,128)(2,1)S(1)} %bitcast.42), channel_id=1, source_target_pairs={{0,32},{32,0},{64,96},{96,64},{128,160},{160,128},{192,224},{224,1... | collective-permute-start | bytes 1179656 | tf_op jit(solution)/shard_map/ppermute | solution.py:133
  100.2 20.2 %copy-start.2 = (f32[128]{0:T(128)S(1)}, f32[128]{0:T(128)}, u32[]{:S(2)}) copy-start(f32[128]{0:T(128)} %param.14) | copy-start | bytes 1540
  100.3 18.0 %collective-permute-start.3 = (bf16[1536,128]{1,0:T(8,128)(2,1)S(1)}, bf16[1536,128]{1,0:T(8,128)(2,1)S(1)}, u32[]{:S(2)}, u32[]{:S(2)}) collective-permute-start(bf16[1536,128]{1,0:T(8,128)(2,1)S(1)} %bitcast.43), channel_id=1, source_target_pairs={{0,1},{1,0},{2,3},{3,2},{4,5},{5,4},{6,7},{7,6},{8,9},{9,8},{10,11... | collective-permute-start | bytes 1179656 | tf_op jit(solution)/shard_map/ppermute | solution.py:132
  104.7 13.5 %collective-permute-start.5 = (f32[100,512]{1,0:T(8,128)S(1)}, f32[100,512]{1,0:T(8,128)S(1)}, u32[]{:S(2)}, u32[]{:S(2)}) collective-permute-start(f32[100,512]{1,0:T(8,128)S(1)} %slice.438), channel_id=1, source_target_pairs={{0,1},{1,0},{2,3},{3,2},{4,5},{5,4},{6,7},{7,6},{8,9},{9,8},{10,11... | collective-permute-start | bytes 614408 | tf_op jit(solution)/shard_map/ppermute | solution.py:77
  118.5 3.6 %collective-permute-start.6 = (bf16[1536,128]{1,0:T(8,128)(2,1)S(1)}, bf16[1536,128]{1,0:T(8,128)(2,1)S(1)}, u32[]{:S(2)}, u32[]{:S(2)}) collective-permute-start(bf16[1536,128]{1,0:T(8,128)(2,1)S(1)} %collective-permute-done.3), channel_id=1, source_target_pairs={{0,32},{32,0},{64,96},{96,64},{128,160},{160,128},{192,224},{224,1... | collective-permute-start | bytes 1179656 | tf_op jit(solution)/shard_map/ppermute | solution.py:148
  125.9 16.6 %collective-permute-start.7 = (bf16[4,256]{1,0:T(4,128)(2,1)S(1)}, bf16[4,256]{1,0:T(4,128)(2,1)S(1)}, u32[]{:S(2)}, u32[]{:S(2)}) collective-permute-start(bf16[4,256]{1,0:T(4,128)(2,1)S(1)} %bitcast.51), channel_id=1, source_target_pairs={{0,0},{1,1},{2,32},{3,33},{4,64},{5,65},{6,96},{7,97},{8,128},{9,1... | collective-permute-start | bytes 6152 | tf_op jit(solution)/shard_map/ppermute | solution.py:173
Sparse Core Ops, SparseCore 0:
  10.1 89.8 all-gather.1

commit v4 on v3

--- a/solution.py
+++ b/solution.py
@@ -154,23 +154,28 @@
     line_pos = line + rows * (line // rows)
     key_pos = jnp.concatenate([line_pos + rows * y, line_pos + rows * (1 - y), step_pos])
 
-    scores = (
-        jnp.einsum("rd,nd->rn", query, cache_keys, preferred_element_type=jnp.float32)
-        * scaling
-    )
-    allowed = key_pos[None, :] <= query_pos[:, None]
-    scores = jnp.where(allowed, scores, -1e30)
-    highest = jnp.max(scores, axis=-1, keepdims=True)
-    weights = jnp.where(allowed, jnp.exp(scores - highest), 0.0)
-    weight_sum = jnp.sum(weights, axis=-1, keepdims=True)
-    summed = jnp.dot(
-        weights.astype(jnp.bfloat16), cache_values, preferred_element_type=jnp.float32
-    )
-    context = (summed / weight_sum).astype(jnp.bfloat16)
-    prompt_context = context[: 4 * rows].reshape(4, rows, HEAD_DIM).transpose(1, 0, 2)
-    step_context = context[4 * rows :].reshape(2, steps, HEAD_DIM).transpose(1, 0, 2)
+    def attend(query, query_pos):
+        scores = (
+            jnp.einsum("rd,nd->rn", query, cache_keys, preferred_element_type=jnp.float32)
+            * scaling
+        )
+        allowed = key_pos[None, :] <= query_pos[:, None]
+        scores = jnp.where(allowed, scores, -1e30)
+        highest = jnp.max(scores, axis=-1, keepdims=True)
+        weights = jnp.where(allowed, jnp.exp(scores - highest), 0.0)
+        weight_sum = jnp.sum(weights, axis=-1, keepdims=True)
+        summed = jnp.dot(
+            weights.astype(jnp.bfloat16), cache_values, preferred_element_type=jnp.float32
+        )
+        return (summed / weight_sum).astype(jnp.bfloat16)
+
+    step_context = attend(query[4 * rows :], query_pos[4 * rows :])
+    step_context, query = lax.optimization_barrier((step_context, query[: 4 * rows]))
+    step_context = step_context.reshape(2, steps, HEAD_DIM).transpose(1, 0, 2)
     half_cols = 2 * HEAD_DIM
     step_out = lax.ppermute(step_context.reshape(steps, half_cols), ("grp", "seq"), STEP_HOME)
+    prompt_context = attend(query, query_pos[: 4 * rows])
+    prompt_context = prompt_context.reshape(4, rows, HEAD_DIM).transpose(1, 0, 2)
     prompt_context = prompt_context.reshape(rows, 4 * HEAD_DIM)
     return (prompt_context, step_out.reshape(steps, 1, half_cols))
 

time: 151 us -> 147 us (0.974)
  the two profiles are of different devices: /device:TPU:16 before, /device:TPU:58 now
where the time goes in v4:
time: 147 us
  blocking collectives  40.5 us (28%)
  waiting for transfers between devices  38.5 us (26%)
  starting transfers between devices  33.4 us (23%)
  between operations  14.5 us (10%)
  other arithmetic  10.1 us (7%)
  matrix products  6.38 us (4%)
  local copies, waits for them, and re-layouts  3.4 us (2%)
    all_gather x1, blocking collectives, gather_z(): lax.all_gather(block, 'seq', axis=0, tiled=True, axis_index_groups=Z_RINGS)  40.5 us
    all_to_all x1, waiting for transfers between devices, shards(): lax.all_to_all(jnp.broadcast_to(kv_type[steps:], (Z, rows, HEAD_DIM)), 's...  18.4 us
    ppermute x2, waiting for transfers between devices, add_halves(): received = lax.ppermute(partial[:rows + steps], 'seq', Y_SWAP)  11.9 us
    all_to_all x1, starting transfers between devices, shards(): lax.all_to_all(jnp.broadcast_to(kv_type[steps:], (Z, rows, HEAD_DIM)), 's...  10.2 us
    ppermute x2, starting transfers between devices, add_halves(): received = lax.ppermute(partial[:rows + steps], 'seq', Y_SWAP)  7.54 us
    ppermute x1, waiting for transfers between devices, shards(): lax.ppermute(step_context.reshape(steps, half_cols), ('grp', 'seq'), STEP...  5.84 us
    ppermute x1, starting transfers between devices, shards(): lax.ppermute(step_context.reshape(steps, half_cols), ('grp', 'seq'), STEP...  5.32 us
  transfers between devices with their start and end apart: 10, of which 6 were waited for; matrix products, arithmetic and copies ran while one was open for 12% of the time, Pallas kernels for 0%

profile of v4, /device:TPU:58, one launch (start us, length us, event | category | flops | bytes accessed | tf_op | source)
XLA Modules:
  0.0 146.8 jit_solution(2774736132066699023)
XLA Ops:
  7.9 1.5 %fusion.7 = f32[96]{0:T(128)S(1)} fusion(bf16[96,5120]{1,0:T(8,128)(2,1)} %param.8), kind=kLoop, calls=%fused_computation.11 | loop fusion | flops 1474464 | bytes 983424 | tf_op jit(solution)/shard_map/reduce_sum | solution.py:27
  9.4 1.5 %fusion.9 = bf16[96,5120]{1,0:T(8,128)(2,1)S(1)} fusion(bf16[96,5120]{1,0:T(8,128)(2,1)} %param.8, f32[5120]{0:T(1024)} %param.10, f32[96]{0:T(128)S(1)} %add_rsqrt_fusion.3), kind=kLoop, calls=%fused_computation.13 | loop fusion | flops 1966080 | bytes 1986944 | tf_op jit(solution)/shard_map/convert_element_type | solution.py:104
  12.3 2.7 %collective-permute-start = (bf16[96,2560]{1,0:T(8,128)(2,1)S(1)}, bf16[96,2560]{1,0:T(8,128)(2,1)S(1)}, u32[]{:S(2)}, u32[]{:S(2)}) collective-permute-start(bf16[96,2560]{1,0:T(8,128)(2,1)S(1)} %concatenate.62), channel_id=1, source_target_pairs={{0,1},{1,0},{2,3},{3,2},{4,5},{5,4},{6,7},{7,6},{8,9},{9,8},{10,11... | collective-permute-start | bytes 1474568 | tf_op jit(solution)/shard_map/ppermute | solution.py:106
  15.0 1.0 dynamic-slice_convert_fusion
  17.2 0.8 dynamic-slice_select_fusion
  18.0 40.5 %all_gather.6 = bf16[2560,128]{1,0:T(8,128)(2,1)S(1)} all-gather(bf16[160,128]{1,0:T(8,128)(2,1)S(1)} %dynamic-slice_select_fusion), channel_id=1, replica_groups={{0,2,4,6,8,10,12,14,16,18,20,22,24,26,28,30},{1,3,5,7,9,11,13,15,17,19,..., dimensions={0}, use_global_device_ids=true | all-gather | bytes 696320 | tf_op jit(solution)/shard_map/all_gather | solution.py:58
  59.2 3.6 %collective-permute-start.1 = (f32[100,128]{1,0:T(8,128)S(1)}, f32[100,128]{1,0:T(8,128)S(1)}, u32[]{:S(2)}, u32[]{:S(2)}) collective-permute-start(f32[100,128]{1,0:T(8,128)S(1)} %slice.434), channel_id=1, source_target_pairs={{0,1},{1,0},{2,3},{3,2},{4,5},{5,4},{6,7},{7,6},{8,9},{9,8},{10,11... | collective-permute-start | bytes 153608 | tf_op jit(solution)/shard_map/ppermute | solution.py:77
  62.9 2.3 %collective-permute-done.1 = f32[100,128]{1,0:T(8,128)S(1)} collective-permute-done((f32[100,128]{1,0:T(8,128)S(1)}, f32[100,128]{1,0:T(8,128)S(1)}, u32[]{:S(2)}, u32[]{:S(2)}) %collective-permute-start.1) | collective-permute-done | bytes 51232 | tf_op jit(solution)/shard_map/ppermute | solution.py:77
  66.6 10.2 %all-to-all-start = ((bf16[16,96,128]{2,1,0:T(8,128)(2,1)}), bf16[16,96,128]{2,1,0:T(8,128)(2,1)S(1)}, u32[]{:S(2)}, u32[]{:S(2)}) async-start(bf16[16,96,128]{2,1,0:T(8,128)(2,1)} %broadcast_in_dim.14), calls=%async_computation | async-start | bytes 786432 | tf_op jit(solution)/shard_map/all_to_all | solution.py:121
  76.9 1.9 %collective-permute-start.2 = (bf16[4,128]{1,0:T(4,128)(2,1)S(1)}, bf16[4,128]{1,0:T(4,128)(2,1)S(1)}, u32[]{:S(2)}, u32[]{:S(2)}) collective-permute-start(bf16[4,128]{1,0:T(4,128)(2,1)S(1)} %slice.440), channel_id=1, source_target_pairs={{0,32},{32,0},{64,96},{96,64},{128,160},{160,128},{192,224},{224,1... | collective-permute-start | bytes 3080 | tf_op jit(solution)/shard_map/ppermute | solution.py:129
  78.9 1.0 collective-permute-done.2
  79.9 18.4 %all-to-all-done = bf16[16,96,128]{2,1,0:T(8,128)(2,1)S(1)} async-done(((bf16[16,96,128]{2,1,0:T(8,128)(2,1)}), bf16[16,96,128]{2,1,0:T(8,128)(2,1)S(1)}, u32[]{:S(2)}, u32[]{:S(2)}) %all-to-all-start) | async-done | bytes 393248 | tf_op jit(solution)/shard_map/all_to_all | solution.py:121
  98.3 1.9 %collective-permute-start.4 = (bf16[1536,128]{1,0:T(8,128)(2,1)S(1)}, bf16[1536,128]{1,0:T(8,128)(2,1)S(1)}, u32[]{:S(2)}, u32[]{:S(2)}) collective-permute-start(bf16[1536,128]{1,0:T(8,128)(2,1)S(1)} %bitcast.43), channel_id=1, source_target_pairs={{0,32},{32,0},{64,96},{96,64},{128,160},{160,128},{192,224},{224,1... | collective-permute-start | bytes 1179656 | tf_op jit(solution)/shard_map/ppermute | solution.py:133
  100.4 1.9 %collective-permute-start.3 = (bf16[1536,128]{1,0:T(8,128)(2,1)S(1)}, bf16[1536,128]{1,0:T(8,128)(2,1)S(1)}, u32[]{:S(2)}, u32[]{:S(2)}) collective-permute-start(bf16[1536,128]{1,0:T(8,128)(2,1)S(1)} %bitcast.44), channel_id=1, source_target_pairs={{0,1},{1,0},{2,3},{3,2},{4,5},{5,4},{6,7},{7,6},{8,9},{9,8},{10,11... | collective-permute-start | bytes 1179656 | tf_op jit(solution)/shard_map/ppermute | solution.py:132
  102.4 2.4 %fusion.55 = f32[196,512]{1,0:T(8,128)S(1)} fusion(bf16[196,2560]{1,0:T(8,128)(2,1)S(1)} %pad_maximum_fusion, bf16[2560,512]{1,0:T(8,128)(2,1)} %all-gather.2.cloned.1.call-done), kind=kOutput, calls=%fused_computation.150 | convolution fusion | flops 513802240 | bytes 4026368 | tf_op jit(solution)/shard_map/dot_general | solution.py:135
  104.9 3.9 %collective-permute-start.5 = (f32[100,512]{1,0:T(8,128)S(1)}, f32[100,512]{1,0:T(8,128)S(1)}, u32[]{:S(2)}, u32[]{:S(2)}) collective-permute-start(f32[100,512]{1,0:T(8,128)S(1)} %slice.442), channel_id=1, source_target_pairs={{0,1},{1,0},{2,3},{3,2},{4,5},{5,4},{6,7},{7,6},{8,9},{9,8},{10,11... | collective-permute-start | bytes 614408 | tf_op jit(solution)/shard_map/ppermute | solution.py:77
  108.8 9.6 %collective-permute-done.5 = f32[100,512]{1,0:T(8,128)S(1)} collective-permute-done((f32[100,512]{1,0:T(8,128)S(1)}, f32[100,512]{1,0:T(8,128)S(1)}, u32[]{:S(2)}, u32[]{:S(2)}) %collective-permute-start.5) | collective-permute-done | bytes 204832 | tf_op jit(solution)/shard_map/ppermute | solution.py:77
  118.7 1.9 %collective-permute-start.6 = (bf16[1536,128]{1,0:T(8,128)(2,1)S(1)}, bf16[1536,128]{1,0:T(8,128)(2,1)S(1)}, u32[]{:S(2)}, u32[]{:S(2)}) collective-permute-start(bf16[1536,128]{1,0:T(8,128)(2,1)S(1)} %collective-permute-done.3), channel_id=1, source_target_pairs={{0,32},{32,0},{64,96},{96,64},{128,160},{160,128},{192,224},{224,1... | collective-permute-start | bytes 1179656 | tf_op jit(solution)/shard_map/ppermute | solution.py:148
  120.7 0.8 fusion.22
  123.4 5.3 %collective-permute-start.7 = (bf16[4,256]{1,0:T(4,128)(2,1)S(1)}, bf16[4,256]{1,0:T(4,128)(2,1)S(1)}, u32[]{:S(2)}, u32[]{:S(2)}) collective-permute-start(bf16[4,256]{1,0:T(4,128)(2,1)S(1)} %bitcast.54), channel_id=1, source_target_pairs={{0,0},{1,1},{2,32},{3,33},{4,64},{5,65},{6,96},{7,97},{8,128},{9,1... | collective-permute-start | bytes 6152 | tf_op jit(solution)/shard_map/ppermute | solution.py:176
  128.7 1.0 fusion.53
  129.8 1.5 %fusion.2 = f32[384]{0:T(512)S(1)} fusion(f32[384,3076]{0,1:T(8,128)S(1)} %get-tuple-element.73, f32[384]{0:T(512)S(1)} %get-tuple-element.72, s32[384]{0:T(512)S(1)} %pad_add_fusion.1, s32[3076]{0:T(1024)S(1)} %pad_add_fusion), kind=kLoop, calls=%fused_computation.5 | loop fusion | flops 4724352 | bytes 4741648 | tf_op jit(solution)/shard_map/reduce_sum | solution.py:166
  131.2 1.7 %fusion.14 = bf16[384,128]{1,0:T(8,128)(2,1)S(1)} fusion(f32[384,3076]{0,1:T(8,128)S(1)} %get-tuple-element.73, f32[384]{0:T(512)S(1)} %get-tuple-element.72, s32[384]{0:T(512)S(1)} %pad_add_fusion.1, s32[3076]{0:T(1024)S(1)} %pad_add_fusion, f32[384]{0:T(512)S(1)} %fusion.2, bf16[3076,128]{1,0:T(8,128)(2,1)S(1)} %constant_dynamic-update-slice_fusion, ...), kind=kOutput, calls=%fused_computation.17 | convolution fusion | flops 309962240 | bytes 6414865 | tf_op jit(solution)/shard_map/dot_general | solution.py:167
  133.6 5.8 %collective-permute-done.7 = bf16[4,256]{1,0:T(4,128)(2,1)S(1)} collective-permute-done((bf16[4,256]{1,0:T(4,128)(2,1)S(1)}, bf16[4,256]{1,0:T(4,128)(2,1)S(1)}, u32[]{:S(2)}, u32[]{:S(2)}) %collective-permute-start.7) | collective-permute-done | bytes 2080 | tf_op jit(solution)/shard_map/ppermute | solution.py:176
  (68 shorter events, 8.9 us)
Async XLA Ops:
  7.2 95.2 %all-gather.2.cloned.1.call-start = ((), (), s32[]{:S(2)}) async-start(), calls=%async_computation.1 | async-start | bytes 2785280 | tf_op jit(solution)/shard_map/all_gather | solution.py:58
  11.4 4.8 %copy-start = (f32[5120]{0:T(1024)S(1)}, f32[5120]{0:T(1024)}, u32[]{:S(2)}) copy-start(f32[5120]{0:T(1024)} %param.10) | copy-start | bytes 61444
  12.3 46.2 %collective-permute-start = (bf16[96,2560]{1,0:T(8,128)(2,1)S(1)}, bf16[96,2560]{1,0:T(8,128)(2,1)S(1)}, u32[]{:S(2)}, u32[]{:S(2)}) collective-permute-start(bf16[96,2560]{1,0:T(8,128)(2,1)S(1)} %concatenate.62), channel_id=1, source_target_pairs={{0,1},{1,0},{2,3},{3,2},{4,5},{5,4},{6,7},{7,6},{8,9},{9,8},{10,11... | collective-permute-start | bytes 1474568 | tf_op jit(solution)/shard_map/ppermute | solution.py:106
  58.6 6.8 %copy-start.1 = (f32[128]{0:T(128)S(1)}, f32[128]{0:T(128)}, u32[]{:S(2)}) copy-start(f32[128]{0:T(128)} %param.15) | copy-start | bytes 1540
  59.2 6.0 %collective-permute-start.1 = (f32[100,128]{1,0:T(8,128)S(1)}, f32[100,128]{1,0:T(8,128)S(1)}, u32[]{:S(2)}, u32[]{:S(2)}) collective-permute-start(f32[100,128]{1,0:T(8,128)S(1)} %slice.434), channel_id=1, source_target_pairs={{0,1},{1,0},{2,3},{3,2},{4,5},{5,4},{6,7},{7,6},{8,9},{9,8},{10,11... | collective-permute-start | bytes 153608 | tf_op jit(solution)/shard_map/ppermute | solution.py:77
  66.6 31.7 %all-to-all-start = ((bf16[16,96,128]{2,1,0:T(8,128)(2,1)}), bf16[16,96,128]{2,1,0:T(8,128)(2,1)S(1)}, u32[]{:S(2)}, u32[]{:S(2)}) async-start(bf16[16,96,128]{2,1,0:T(8,128)(2,1)} %broadcast_in_dim.14), calls=%async_computation | async-start | bytes 786432 | tf_op jit(solution)/shard_map/all_to_all | solution.py:121
  76.9 3.0 %collective-permute-start.2 = (bf16[4,128]{1,0:T(4,128)(2,1)S(1)}, bf16[4,128]{1,0:T(4,128)(2,1)S(1)}, u32[]{:S(2)}, u32[]{:S(2)}) collective-permute-start(bf16[4,128]{1,0:T(4,128)(2,1)S(1)} %slice.440), channel_id=1, source_target_pairs={{0,32},{32,0},{64,96},{96,64},{128,160},{160,128},{192,224},{224,1... | collective-permute-start | bytes 3080 | tf_op jit(solution)/shard_map/ppermute | solution.py:129
  98.3 4.0 %collective-permute-start.4 = (bf16[1536,128]{1,0:T(8,128)(2,1)S(1)}, bf16[1536,128]{1,0:T(8,128)(2,1)S(1)}, u32[]{:S(2)}, u32[]{:S(2)}) collective-permute-start(bf16[1536,128]{1,0:T(8,128)(2,1)S(1)} %bitcast.43), channel_id=1, source_target_pairs={{0,32},{32,0},{64,96},{96,64},{128,160},{160,128},{192,224},{224,1... | collective-permute-start | bytes 1179656 | tf_op jit(solution)/shard_map/ppermute | solution.py:133
  100.4 18.0 %collective-permute-start.3 = (bf16[1536,128]{1,0:T(8,128)(2,1)S(1)}, bf16[1536,128]{1,0:T(8,128)(2,1)S(1)}, u32[]{:S(2)}, u32[]{:S(2)}) collective-permute-start(bf16[1536,128]{1,0:T(8,128)(2,1)S(1)} %bitcast.44), channel_id=1, source_target_pairs={{0,1},{1,0},{2,3},{3,2},{4,5},{5,4},{6,7},{7,6},{8,9},{9,8},{10,11... | collective-permute-start | bytes 1179656 | tf_op jit(solution)/shard_map/ppermute | solution.py:132
  104.8 15.8 %copy-start.2 = (f32[128]{0:T(128)S(1)}, f32[128]{0:T(128)}, u32[]{:S(2)}) copy-start(f32[128]{0:T(128)} %param.14) | copy-start | bytes 1540
  104.9 13.5 %collective-permute-start.5 = (f32[100,512]{1,0:T(8,128)S(1)}, f32[100,512]{1,0:T(8,128)S(1)}, u32[]{:S(2)}, u32[]{:S(2)}) collective-permute-start(f32[100,512]{1,0:T(8,128)S(1)} %slice.442), channel_id=1, source_target_pairs={{0,1},{1,0},{2,3},{3,2},{4,5},{5,4},{6,7},{7,6},{8,9},{9,8},{10,11... | collective-permute-start | bytes 614408 | tf_op jit(solution)/shard_map/ppermute | solution.py:77
  118.7 3.6 %collective-permute-start.6 = (bf16[1536,128]{1,0:T(8,128)(2,1)S(1)}, bf16[1536,128]{1,0:T(8,128)(2,1)S(1)}, u32[]{:S(2)}, u32[]{:S(2)}) collective-permute-start(bf16[1536,128]{1,0:T(8,128)(2,1)S(1)} %collective-permute-done.3), channel_id=1, source_target_pairs={{0,32},{32,0},{64,96},{96,64},{128,160},{160,128},{192,224},{224,1... | collective-permute-start | bytes 1179656 | tf_op jit(solution)/shard_map/ppermute | solution.py:148
  123.4 16.0 %collective-permute-start.7 = (bf16[4,256]{1,0:T(4,128)(2,1)S(1)}, bf16[4,256]{1,0:T(4,128)(2,1)S(1)}, u32[]{:S(2)}, u32[]{:S(2)}) collective-permute-start(bf16[4,256]{1,0:T(4,128)(2,1)S(1)} %bitcast.54), channel_id=1, source_target_pairs={{0,0},{1,1},{2,32},{3,33},{4,64},{5,65},{6,96},{7,97},{8,128},{9,1... | collective-permute-start | bytes 6152 | tf_op jit(solution)/shard_map/ppermute | solution.py:176
Sparse Core Ops, SparseCore 0:
  10.1 89.5 all-gather.1
